TPU v7x, 32 devices: a whole 2x2x4 slice. The times are simulated.
32 devices in a mesh: ctx: 8 (over z, core), head: 4 (over y, x).
Axes of the slice: x: 2, y: 2, z: 4, core: 2. Of those that a mesh axis runs over, the one named last changes fastest.
Arguments:
- hidden_in: bfloat16 [2048, 8192], P('ctx', 'head'), may hold values from -90 to 90
- query_rows: bfloat16 [2048, 8192], P('ctx', 'head'), may hold values from -5 to 5
- key_rows: bfloat16 [2048, 1024], P('ctx', 'head'), may hold values from -5 to 5
- value_rows: bfloat16 [2048, 1024], P('ctx', 'head'), may hold values from -6 to 6
- out_weight: bfloat16 [8192, 8192], P('head'), may hold values from -0.0625 to 0.0625
- grad_out: bfloat16 [2048, 8192], P('ctx', 'head'), may hold values from -6 to 6
- answer_mask: int32 [2048], P('ctx'), may hold values 0 or 1
Outputs:
- grad_query: bfloat16 [2048, 8192], P('ctx', 'head')
- grad_key: bfloat16 [2048, 1024], P('ctx', 'head')
- grad_value: bfloat16 [2048, 1024], P('ctx', 'head')
- fisher_q: float32 [8, 64], P('ctx', 'head')
- fisher_o: float32 [8, 64], P('ctx', 'head')
All inputs are finite; a program needn't handle non-finite values. No bound on the sum of `answer_mask` on one device may be relied on, other than what follows from the above.
Results may differ from a plain program's by a relative error of at most 0.019.
Values may be sent and summed in bfloat16 or wider, within the bound.
A program may use at most 128 MiB of HBM per device.

v0:
```python
import math

import jax
import jax.numpy as jnp
from jax import lax
from jax.sharding import PartitionSpec as P

D = 8192
HEADS = 64
KVH = 8
HD = 128


NEGATIVE = -1e30
EPSILON = 1e-06


def block_scores(query_group, key_block, scaling, row_pos, col_pos):
    scores = (
        jnp.einsum("tgd,kd->tgk", query_group, key_block, preferred_element_type=jnp.float32)
        * scaling
    )
    return jnp.where(row_pos[:, None, None] >= col_pos[None, None, :], scores, NEGATIVE)


def head_squares(left_side, right_side, head_dim):
    product = lax.dot_general(
        left_side, right_side, (((0,), (0,)), ((), ())), preferred_element_type=jnp.float32
    )
    shaped = (product * product).reshape(
        product.shape[0], right_side.shape[1] // head_dim, head_dim
    )
    return jnp.sum(shaped, axis=(0, 2))


def body(hidden_in, query_rows, key_rows, value_rows, out_weight, grad_out, answer_mask):
    tok_dev = query_rows.shape[0]
    head_dim = HD
    group_size = HEADS // KVH
    local_groups = key_rows.shape[1] // head_dim
    scaling = head_dim ** (-0.5)
    own_index = lax.axis_index("ctx")
    first_row = own_index * tok_dev
    loss_weight = 0.25 + answer_mask.astype(jnp.float32)
    weighted = (grad_out.astype(jnp.float32) * loss_weight[:, None]).astype(jnp.bfloat16)
    keys_all, values_all = (
        lax.all_gather(key_rows, "ctx", axis=0, tiled=True),
        lax.all_gather(value_rows, "ctx", axis=0, tiled=True),
    )
    tokens = keys_all.shape[0]
    block_rows = math.gcd(512, tokens)

    def fetch(table, group_index, block_number):
        column = table[:, group_index * head_dim : (group_index + 1) * head_dim]
        return lax.dynamic_slice_in_dim(column, block_number * block_rows, block_rows, 0)

    def column_pos(block_number):
        return block_number * block_rows + jnp.arange(block_rows, dtype=jnp.int32)

    buffer = jnp.zeros((tokens, 2 * local_groups * head_dim), jnp.float32)
    rows = query_rows.shape[0]
    row_pos = first_row + jnp.arange(rows, dtype=jnp.int32)
    needed = (first_row + rows - 1) // block_rows + 1
    query_heads = query_rows.reshape(rows, local_groups, group_size, head_dim)
    log_totals = []
    attended_list = []
    for shared_head in range(local_groups):
        query_group = query_heads[:, shared_head]

        def stats_step(block_number, carried):
            running_max, running_sum = carried
            key_block = fetch(keys_all, shared_head, block_number)
            scores = block_scores(
                query_group, key_block, scaling, row_pos, column_pos(block_number)
            )
            new_max = jnp.maximum(running_max, jnp.max(scores, axis=-1))
            running_sum = running_sum * jnp.exp(running_max - new_max) + jnp.sum(
                jnp.exp(scores - new_max[..., None]), axis=-1
            )
            return (new_max, running_sum)

        start_max = jnp.full((rows, group_size), NEGATIVE, jnp.float32)
        start_sum = jnp.zeros((rows, group_size), jnp.float32)
        running_max, running_sum = lax.fori_loop(0, needed, stats_step, (start_max, start_sum))
        log_total = running_max + jnp.log(running_sum)

        def value_step(block_number, accumulated):
            key_block = fetch(keys_all, shared_head, block_number)
            value_block = fetch(values_all, shared_head, block_number)
            scores = block_scores(
                query_group, key_block, scaling, row_pos, column_pos(block_number)
            )
            rounded = jnp.exp(scores - log_total[..., None]).astype(jnp.bfloat16)
            return accumulated + jnp.einsum(
                "tgk,kd->tgd", rounded, value_block, preferred_element_type=jnp.float32
            )

        accumulated = lax.fori_loop(
            0, needed, value_step, jnp.zeros((rows, group_size, head_dim), jnp.float32)
        )
        log_totals.append(log_total)
        attended_list.append(accumulated.astype(jnp.bfloat16))
    attended_part = jnp.stack(attended_list, axis=1).reshape(
        rows, local_groups * group_size * head_dim
    )
    log_totals, attended = (log_totals, attended_part)
    piece_part = lax.all_gather(weighted, "head", axis=1, tiled=True)
    grad_sum = lax.dot_general(
        piece_part, out_weight, (((1,), (1,)), ((), ())), preferred_element_type=jnp.float32
    )
    grad_sum, squares_out = (grad_sum, head_squares(piece_part, attended, head_dim))
    grad_attended, squares_out = (grad_sum.astype(jnp.bfloat16), squares_out)
    backward_buffer = buffer
    rows = query_rows.shape[0]
    backward_row_pos = first_row + jnp.arange(rows, dtype=jnp.int32)
    needed = (first_row + rows - 1) // block_rows + 1
    query_heads = query_rows.reshape(rows, local_groups, group_size, head_dim)
    grad_heads = grad_attended.reshape(rows, local_groups, group_size, head_dim)
    attended_heads = attended.reshape(rows, local_groups, group_size, head_dim)
    query_grads = []
    for backward_shared_head in range(local_groups):
        backward_query_group = query_heads[:, backward_shared_head]
        grad_group = grad_heads[:, backward_shared_head]
        backward_log_total = log_totals[backward_shared_head]
        row_dot = jnp.sum(
            grad_group.astype(jnp.float32)
            * attended_heads[:, backward_shared_head].astype(jnp.float32),
            axis=-1,
        )
        key_column = jnp.int32(backward_shared_head * head_dim)
        value_column = jnp.int32((local_groups + backward_shared_head) * head_dim)

        def back_step(block_number, carried):
            query_sum, buffer_now = carried
            key_block = fetch(keys_all, backward_shared_head, block_number)
            value_block = fetch(values_all, backward_shared_head, block_number)
            scores = block_scores(
                backward_query_group, key_block, scaling, backward_row_pos, column_pos(block_number)
            )
            softmax = jnp.exp(scores - backward_log_total[..., None])
            rounded = softmax.astype(jnp.bfloat16)
            grad_prob = jnp.einsum(
                "tgd,kd->tgk", grad_group, value_block, preferred_element_type=jnp.float32
            )
            grad_score = (softmax * (grad_prob - row_dot[..., None]) * scaling).astype(jnp.bfloat16)
            query_sum = query_sum + jnp.einsum(
                "tgk,kd->tgd", grad_score, key_block, preferred_element_type=jnp.float32
            )
            key_part = jnp.einsum(
                "tgk,tgd->kd", grad_score, backward_query_group, preferred_element_type=jnp.float32
            )
            value_part = jnp.einsum(
                "tgk,tgd->kd", rounded, grad_group, preferred_element_type=jnp.float32
            )
            row_start = (block_number * block_rows).astype(jnp.int32)
            old_key = lax.dynamic_slice(buffer_now, (row_start, key_column), (block_rows, head_dim))
            buffer_now = lax.dynamic_update_slice(
                buffer_now, old_key + key_part, (row_start, key_column)
            )
            old_value = lax.dynamic_slice(
                buffer_now, (row_start, value_column), (block_rows, head_dim)
            )
            buffer_now = lax.dynamic_update_slice(
                buffer_now, old_value + value_part, (row_start, value_column)
            )
            return (query_sum, buffer_now)

        start_query = jnp.zeros((rows, group_size, head_dim), jnp.float32)
        query_sum, backward_buffer = lax.fori_loop(
            0, needed, back_step, (start_query, backward_buffer)
        )
        query_grads.append(query_sum.astype(jnp.bfloat16))
    grad_query_part = jnp.stack(query_grads, axis=1).reshape(
        rows, local_groups * group_size * head_dim
    )
    key_sums = lax.psum_scatter(
        backward_buffer.astype(jnp.bfloat16), "ctx", scatter_dimension=0, tiled=True
    ).astype(jnp.float32)
    grad_key = key_sums[:, : local_groups * head_dim].astype(jnp.bfloat16)
    grad_value = key_sums[:, local_groups * head_dim :].astype(jnp.bfloat16)
    squares_query = head_squares(
        lax.all_gather(hidden_in, "head", axis=1, tiled=True), grad_query_part, head_dim
    )
    normal_size = D * head_dim * tok_dev
    fisher_q = jnp.log(squares_query / normal_size + EPSILON).reshape(1, -1)
    fisher_o = jnp.log(squares_out / normal_size + EPSILON).reshape(1, -1)
    return (grad_query_part, grad_key, grad_value, fisher_q, fisher_o)


def solution(mesh):
    return jax.shard_map(
        body,
        mesh=mesh,
        in_specs=(
            P("ctx", "head"),
            P("ctx", "head"),
            P("ctx", "head"),
            P("ctx", "head"),
            P("head", None),
            P("ctx", "head"),
            P("ctx"),
        ),
        out_specs=(
            P("ctx", "head"),
            P("ctx", "head"),
            P("ctx", "head"),
            P("ctx", "head"),
            P("ctx", "head"),
        ),
        check_vma=False,
    )
```

profile of v0, /device:TPU:0, one launch (start us, length us, event | category | flops | bytes accessed | tf_op | source)
XLA Modules:
  0.0 260.7 jit_solution(7204399221081822716)
XLA Ops:
  9.4 2.5 multiply_convert_fusion
  13.7 20.7 %all-gather.5.cloned.1.call-done = bf16[2048,256]{1,0:T(8,128)(2,1)} async-done(((bf16[256,256]{1,0:T(8,128)(2,1)}), bf16[2048,256]{1,0:T(8,128)(2,1)}) %all-gather.5.cloned.1.call-update) | async-done | bytes 1048592 | tf_op jit(solution)/shard_map/all_gather | solution.py:47
  34.4 2.9 %while.77 = (s32[]{:T(128)}, f32[256,8]{0,1:T(8,128)S(1)}, f32[256,8]{0,1:T(8,128)S(1)}, s32[]{:T(128)}, bf16[2048,256]{1,0:T(8,128)(2,1)}, /*index=5*/bf16[256,...) while((s32[]{:T(128)}, f32[256,8]{0,1:T(8,128)S(1)}, ...), condition=%wide.region_12.13_spmd.clone, body=%wide.region_9.12_spmd.clone.sunk | while | flops 275911424 | bytes 10598567 | solution.py:84
  37.4 3.0 %while.74 = (s32[]{:T(128)}, f32[256,8]{0,1:T(8,128)S(1)}, f32[256,8]{0,1:T(8,128)S(1)}, s32[]{:T(128)}, bf16[2048,256]{1,0:T(8,128)(2,1)}, /*index=5*/bf16[256,...) while((s32[]{:T(128)}, f32[256,8]{0,1:T(8,128)S(1)}, ...), condition=%wide.region_3.4_spmd.clone, body=%wide.region_0.3_spmd.clone.sunk | while | flops 275911424 | bytes 10598567 | solution.py:84
  37.6 1.1 slice.94
  40.4 17.4 %all-gather.7.cloned.1.call-done = bf16[2048,256]{1,0:T(8,128)(2,1)} async-done(((bf16[256,256]{1,0:T(8,128)(2,1)}), bf16[2048,256]{1,0:T(8,128)(2,1)}) %all-gather.7.cloned.1.call-update) | async-done | bytes 1048592 | tf_op jit(solution)/shard_map/all_gather | solution.py:48
  57.9 4.1 %while.75 = (s32[]{:T(128)}, f32[256,8,128]{2,0,1:T(8,128)S(1)}, s32[]{:T(128)}, bf16[2048,256]{1,0:T(8,128)(2,1)}, bf16[256,8,128]{2,0,1:T(8,128)(2,1)S(1)}, /*...) while((s32[]{:T(128)}, f32[256,8,128]{2,0,1:T(8,128)S(1)}, ...), condition=%wide.region_5.6_spmd.clone, body=%wide.region_4.5_spmd.clone.sunk | while | flops 541459200 | bytes 5258411 | solution.py:98
  60.2 1.7 fusion.182
  63.3 6.3 %while.78 = (s32[]{:T(128)}, f32[256,8,128]{2,0,1:T(8,128)}, s32[]{:T(128)}, bf16[2048,256]{1,0:T(8,128)(2,1)}, bf16[256,8,128]{2,0,1:T(8,128)(2,1)S(1)}, /*inde...) while((s32[]{:T(128)}, f32[256,8,128]{2,0,1:T(8,128)}, ...), condition=%wide.region_14.15_spmd.clone, body=%wide.region_13.14_spmd.clone.sunk | while | flops 541459200 | bytes 5258411 | solution.py:98
  65.6 4.0 %fusion.202 = f32[256,8,128]{2,0,1:T(8,128)} fusion(f32[256,8,128]{2,0,1:T(8,128)} %get-tuple-element.1072, bf16[256,8,128]{2,0,1:T(8,128)(2,1)S(1)} %get-tuple-element.1087, f32[256,8]{0,1:T(8,128)S(1)} %get-tuple-element.1088, pred[256,512]{0,1:T(8,128)(4,1)S(1)} %broadcast_compare_fusion.16, bf16[2048,128]{1,0:T(8,128)(2,1)S(1)} %slice.100, ...), kind=kOutput, calls=%fused_computation.80.clone.1 | convolution fusion | flops 541327360 | bytes 3023872 | tf_op jit(solution)/shard_map/while/body/tgk,kd->tgd/dot_general | solution.py:94
  69.5 1.4 copy.49
  71.0 1.1 pad_maximum_fusion.1
  72.1 40.0 %all-gather.9.cloned.1.call-done = bf16[256,8192]{1,0:T(8,128)(2,1)} async-done(((bf16[256,2048]{1,0:T(8,128)(2,1)}), bf16[256,8192]{1,0:T(8,128)(2,1)}) %all-gather.9.cloned.1.call-update) | async-done | bytes 4194320 | tf_op jit(solution)/shard_map/all_gather | solution.py:107
  112.0 17.5 %convolution_convert_fusion = bf16[256,2048]{1,0:T(8,128)(2,1)} fusion(bf16[256,8192]{1,0:T(8,128)(2,1)} %all-gather.9.cloned.1.call-done, bf16[2048,8192]{1,0:T(8,128)(2,1)} %param.23), kind=kOutput, calls=%fused_computation.124 | convolution fusion | flops 8590458880 | bytes 38797312 | tf_op jit(solution)/shard_map/dot_general | solution.py:108
  129.6 1.5 copy.57
  132.4 2.2 copy.51
  134.6 2.0 copy.45
  137.7 2.5 broadcast_in_dim.76
  140.2 8.9 %while.76 = (s32[]{:T(128)}, f32[256,8,128]{2,0,1:T(8,128)}, f32[2048,512]{1,0:T(8,128)}, s32[]{:T(128)}, bf16[2048,256]{1,0:T(8,128)(2,1)S(1)}, /*index=5*/bf16...) while((s32[]{:T(128)}, f32[256,8,128]{2,0,1:T(8,128)}, ...), condition=%wide.region_8.9_spmd.clone, body=%wide.region_7.8_spmd.clone.sunk | while | flops 1354236672 | bytes 37517608 | solution.py:169
  141.2 1.5 fusion.194
  143.7 2.6 %fusion.195 = f32[2048,512]{1,0:T(8,128)} fusion(f32[2048,512]{1,0:T(8,128)} %get-tuple-element.1148, s32[]{:T(128)S(6)} %select_n.155, bf16[256,8,512]{0,2,1:T(8,128)(2,1)S(1)} %fusion.194, bf16[256,8,128]{2,0,1:T(8,128)(2,1)S(1)} %get-tuple-element.1166), kind=kOutput, calls=%fused_computation.48.clone.1 | convolution fusion | flops 268500992 | bytes 3145732 | tf_op jit(solution)/shard_map/while/body/tgk,tgd->kd/dot_general | solution.py:149
  146.3 2.8 %fusion.196 = f32[2048,512]{1,0:T(8,128)} fusion(f32[2048,512]{1,0:T(8,128)} %fusion.195, s32[]{:T(128)S(6)} %select_n.155, bf16[256,8,128]{2,0,1:T(8,128)(2,1)S(1)} %copy-done.12, f32[512,256,8]{1,0,2:T(8,128)S(1)} %fusion.193, f32[256,8]{0,1:T(8,128)S(1)} %get-tuple-element.1167, pred[256,512]{0,1:T(8,128)(4,1)S(1)} %broadcast_compare_fusion.14), kind=kOutput, calls=%fused_computation.46.clone.1 | convolution fusion | flops 272695296 | bytes 5382148 | tf_op jit(solution)/shard_map/while/body/tgk,tgd->kd/dot_general | solution.py:152
  150.2 8.9 %while.79 = (s32[]{:T(128)}, f32[256,8,128]{2,0,1:T(8,128)}, f32[2048,512]{1,0:T(8,128)}, s32[]{:T(128)}, bf16[2048,256]{1,0:T(8,128)(2,1)S(1)}, /*index=5*/bf16...) while((s32[]{:T(128)}, f32[256,8,128]{2,0,1:T(8,128)}, ...), condition=%wide.region_17.18_spmd.clone, body=%wide.region_16.17_spmd.clone.sunk | while | flops 1354236672 | bytes 37517608 | solution.py:169
  151.2 1.5 fusion.214
  153.7 2.6 %fusion.215 = f32[2048,512]{1,0:T(8,128)} fusion(f32[2048,512]{1,0:T(8,128)} %get-tuple-element.1193, s32[]{:T(128)S(6)} %select_n.163, bf16[256,8,512]{0,2,1:T(8,128)(2,1)S(1)} %fusion.214, bf16[256,8,128]{2,0,1:T(8,128)(2,1)S(1)} %get-tuple-element.1211), kind=kOutput, calls=%fused_computation.106.clone.1 | convolution fusion | flops 268500992 | bytes 3145732 | tf_op jit(solution)/shard_map/while/body/tgk,tgd->kd/dot_general | solution.py:149
  156.3 2.8 %fusion.216 = f32[2048,512]{1,0:T(8,128)} fusion(f32[2048,512]{1,0:T(8,128)} %fusion.215, s32[]{:T(128)S(6)} %select_n.163, bf16[256,8,128]{2,0,1:T(8,128)(2,1)S(1)} %copy-done.11, f32[512,256,8]{1,0,2:T(8,128)S(1)} %fusion.213, f32[256,8]{0,1:T(8,128)S(1)} %get-tuple-element.1212, pred[256,512]{0,1:T(8,128)(4,1)S(1)} %broadcast_compare_fusion.17), kind=kOutput, calls=%fused_computation.104.clone.1 | convolution fusion | flops 272695296 | bytes 5382148 | tf_op jit(solution)/shard_map/while/body/tgk,tgd->kd/dot_general | solution.py:152
  159.1 3.9 %convert_element_type.72 = bf16[2048,512]{1,0:T(8,128)(2,1)} convert(f32[2048,512]{1,0:T(8,128)} %get-tuple-element.296) | non-fusion elementwise | flops 1048576 | bytes 6291456 | tf_op jit(solution)/shard_map/convert_element_type | solution.py:177
  164.3 1.7 copy-done.13
  166.0 9.2 %multiply_reduce_fusion = f32[2048]{0:T(1024)S(1)} fusion(bf16[256,8192]{1,0:T(8,128)(2,1)S(1)} %copy-done.13, bf16[256,2048]{0,1:T(8,128)(2,1)S(1)} %bitcast.300), kind=kOutput, calls=%fused_computation.122 | convolution fusion | flops 8623486976 | bytes 5251072 | tf_op jit(solution)/shard_map/dot_general | solution.py:27
  175.4 12.1 %multiply_reduce_fusion.1 = f32[2048]{0:T(1024)S(1)} fusion(bf16[256,2048]{1,0:T(8,128)(2,1)S(1)} %bitcast.301, bf16[256,8192]{1,0:T(8,128)(2,1)} %all-gather.11.cloned.1.call-done), kind=kOutput, calls=%fused_computation.123 | convolution fusion | flops 8623486976 | bytes 5251072 | tf_op jit(solution)/shard_map/dot_general | solution.py:27
  188.6 63.9 %reduce-scatter.2.cloned.1.call-done = bf16[256,512]{1,0:T(8,128)(2,1)} async-done(((bf16[2048,512]{1,0:T(8,128)(2,1)}), bf16[256,512]{1,0:T(8,128)(2,1)}) %reduce-scatter.2.cloned.1.call-update) | async-done | bytes 262160 | tf_op jit(solution)/shard_map/reduce_scatter | solution.py:176
  252.5 1.7 fusion.114
  (106 shorter events, 24.5 us)
Async XLA Ops:
  7.2 5.4 %copy-start.8 = (bf16[256,2048]{1,0:T(8,128)(2,1)S(1)}, bf16[256,2048]{1,0:T(8,128)(2,1)}, u32[]{:S(2)}) copy-start(bf16[256,2048]{1,0:T(8,128)(2,1)} %param.20) | copy-start | bytes 3145732
  7.2 27.3 %all-gather.5.cloned.1.call-start = ((), (), s32[]{:S(2)}) async-start(), calls=%async_computation.1 | async-start | bytes 1179648 | tf_op jit(solution)/shard_map/all_gather | solution.py:47
  7.9 49.9 %all-gather.7.cloned.1.call-start = ((), (), s32[]{:S(2)}) async-start(), calls=%async_computation.2 | async-start | bytes 1179648 | tf_op jit(solution)/shard_map/all_gather | solution.py:48
  8.7 103.4 %all-gather.9.cloned.1.call-start = ((), (), s32[]{:S(2)}) async-start(), calls=%async_computation.3 | async-start | bytes 5242880 | tf_op jit(solution)/shard_map/all_gather | solution.py:107
  11.9 163.4 %all-gather.11.cloned.1.call-start = ((), (), s32[]{:S(2)}) async-start(), calls=%async_computation.5 | async-start | bytes 5242880 | tf_op jit(solution)/shard_map/all_gather | solution.py:182
  12.5 240.0 %reduce-scatter.2.cloned.1.call-start = ((), (), s32[]{:S(2)}) async-start(), calls=%async_computation.4 | async-start | bytes 2359296 | tf_op jit(solution)/shard_map/reduce_scatter | solution.py:176
  132.4 7.8 %copy-start = (bf16[2048,256]{1,0:T(8,128)(2,1)S(1)}, bf16[2048,256]{1,0:T(8,128)(2,1)}, u32[]{:S(2)}) copy-start(bf16[2048,256]{1,0:T(8,128)(2,1)} %get-tuple-element.1230) | copy-start | bytes 3145732
  132.4 7.8 %copy-start.1 = (bf16[2048,256]{1,0:T(8,128)(2,1)S(1)}, bf16[2048,256]{1,0:T(8,128)(2,1)}, u32[]{:S(2)}) copy-start(bf16[2048,256]{1,0:T(8,128)(2,1)} %get-tuple-element.1238) | copy-start | bytes 3145732
  140.2 1.0 copy-start.12
  141.2 1.5 copy-start.5
  143.7 5.4 %copy-start.6 = (f32[256,8,128]{2,0,1:T(8,128)}, f32[256,8,128]{2,0,1:T(8,128)S(1)}, u32[]{:S(2)}) copy-start(f32[256,8,128]{2,0,1:T(8,128)S(1)} %convolution_add_fusion.4) | copy-start | bytes 3145732 | tf_op jit(solution)/shard_map/while
  150.2 1.0 copy-start.11
  151.2 1.5 copy-start.2
  153.6 5.4 %copy-start.3 = (f32[256,8,128]{2,0,1:T(8,128)}, f32[256,8,128]{2,0,1:T(8,128)S(1)}, u32[]{:S(2)}) copy-start(f32[256,8,128]{2,0,1:T(8,128)S(1)} %convolution_add_fusion.5) | copy-start | bytes 3145732 | tf_op jit(solution)/shard_map/while
  159.1 3.9 %copy-start.4 = (f32[256,8,128]{2,0,1:T(8,128)S(1)}, f32[256,8,128]{2,0,1:T(8,128)}, u32[]{:S(2)}) copy-start(f32[256,8,128]{2,0,1:T(8,128)} %get-tuple-element.295) | copy-start | bytes 3145732
  159.1 4.1 %copy-start.7 = (f32[256,8,128]{2,0,1:T(8,128)S(1)}, f32[256,8,128]{2,0,1:T(8,128)}, u32[]{:S(2)}) copy-start(f32[256,8,128]{2,0,1:T(8,128)} %get-tuple-element.290) | copy-start | bytes 3145732
  163.1 1.2 copy-start.9
  163.1 2.9 %copy-start.13 = (bf16[256,8192]{1,0:T(8,128)(2,1)S(1)}, bf16[256,8192]{1,0:T(8,128)(2,1)}, u32[]{:S(2)}) copy-start(bf16[256,8192]{1,0:T(8,128)(2,1)} %all-gather.9.cloned.1.call-done) | copy-start | bytes 12582916
  164.3 11.1 %copy-start.10 = (bf16[32,8,16,128]{3,1,2,0:T(8,128)(2,1)}, bf16[32,8,16,128]{3,1,2,0:T(8,128)(2,1)S(1)}, u32[]{:S(2)}) copy-start(bf16[32,8,16,128]{3,1,2,0:T(8,128)(2,1)S(1)} %copy.60) | copy-start | bytes 3145732
Sparse Core Ops, SparseCore 0:
  9.6 24.7 all-gather.4
  36.0 21.7 all-gather.6
  59.7 52.3 all-gather.8
  113.7 52.7 all-gather.10
  168.6 83.8 reduce-scatter.1
where the time goes:
time: 263 us; the launch traced here: 261 us
  waiting for transfers between devices  144 us (55%)
  matrix products  63.2 us (24%)
  local copies, waits for them, and re-layouts  26.4 us (10%)
  between operations  14 us (5%)
  other arithmetic  12.7 us (5%)
    reduce_scatter x1, waiting for transfers between devices, body(): lax.psum_scatter(backward_buffer.astype(jnp.bfloat16), 'ctx', scatter_dim...  63.9 us
    all_gather x1, waiting for transfers between devices, body(): piece_part = lax.all_gather(weighted, 'head', axis=1, tiled=True)  40 us
    dot_general x2, matrix products, head_squares(): lax.dot_general(left_side, right_side, (((0,), (0,)), ((), ())), preferre...  21.3 us
    all_gather x1, waiting for transfers between devices, body(): lax.all_gather(key_rows, 'ctx', axis=0, tiled=True)  20.7 us
    dot_general x1, matrix products, body(): lax.dot_general(piece_part, out_weight, (((1,), (1,)), ((), ())), preferr...  17.5 us
    all_gather x1, waiting for transfers between devices, body(): lax.all_gather(value_rows, 'ctx', axis=0, tiled=True)  17.4 us
    unnamed x22, local copies, waits for them, and re-layouts  7.31 us
    slice x10, local copies, waits for them, and re-layouts, fetch(): column = table[:, group_index * head_dim:(group_index + 1) * head_dim]  6.61 us
  transfers between devices with their start and end apart: 5, of which 4 were waited for; matrix products, arithmetic and copies ran while one was open for 38% of the time, Pallas kernels for 0%

commit v1 on v0

v1 whole, which is shorter than its diff:
```python
import functools

import jax
import jax.numpy as jnp
from jax import lax
from jax.experimental import pallas as pl
from jax.experimental.pallas import tpu as pltpu
from jax.sharding import PartitionSpec as P

HD = 128
GROUP = 8
NEGATIVE = -1e30
EPSILON = 1e-06
SCALING = HD ** (-0.5)
LOG2E = 1.4426950408889634
SCALE2 = SCALING * LOG2E
VMEM_LIMIT = 56 * 1024 * 1024


def dot(left, right, left_dim, right_dim):
    return lax.dot_general(
        left, right, (((left_dim,), (right_dim,)), ((), ())), preferred_element_type=jnp.float32
    )


def columns(index):
    return pl.ds(pl.multiple_of(index * HD, HD), HD)


def causal_keep(rows):
    key_pos = lax.broadcasted_iota(jnp.int32, (rows, rows), 0)
    query_pos = lax.broadcasted_iota(jnp.int32, (rows, rows), 1)
    return key_pos <= query_pos


def forward_kernel(groups, query_ref, kv_ref, attended_ref, log_ref, sum_ref, max_ref, total_ref):
    rows = query_ref.shape[0]
    own = lax.axis_index("ctx")

    def block(number, diagonal):
        row_at = pl.ds(pl.multiple_of(number * rows, rows), rows)

        def one_group(group, _):
            key_block = kv_ref[row_at, columns(group)]
            value_turned = kv_ref[row_at, columns(groups + group)].T
            for member in range(GROUP):
                head = group * GROUP + member
                scores = dot(key_block, query_ref[:, columns(head)], 1, 1)
                one = pl.ds(head, 1)
                if diagonal:
                    scores = jnp.where(causal_keep(rows), scores, NEGATIVE)
                    new_max = jnp.max(scores, axis=0, keepdims=True)
                else:
                    old_max = max_ref[one, :]
                    new_max = jnp.maximum(old_max, jnp.max(scores, axis=0, keepdims=True))
                weights = jnp.exp2(scores * SCALE2 - new_max * SCALE2)
                weights_sum = jnp.sum(weights, axis=0, keepdims=True)
                part = dot(value_turned, weights.astype(jnp.bfloat16), 1, 0)
                if diagonal:
                    total_ref[one, :] = weights_sum
                    sum_ref[columns(head), :] = part
                else:
                    factor = jnp.exp2((old_max - new_max) * SCALE2)
                    total_ref[one, :] = total_ref[one, :] * factor + weights_sum
                    sum_ref[columns(head), :] = sum_ref[columns(head), :] * factor + part
                max_ref[one, :] = new_max
            return 0

        lax.fori_loop(0, groups, one_group, 0)

    block(own, True)

    def step(number, _):
        block(number, False)
        return 0

    lax.fori_loop(0, own, step, 0)
    for head in range(groups * GROUP):
        total = total_ref[head : head + 1, :]
        log_ref[head : head + 1, :] = max_ref[head : head + 1, :] * SCALE2 + jnp.log2(total)
        part = sum_ref[head * HD : (head + 1) * HD, :]
        attended_ref[head * HD : (head + 1) * HD, :] = (part / total).astype(jnp.bfloat16)


def backward_kernel(
    groups,
    query_ref,
    kv_ref,
    grad_ref,
    attended_ref,
    log_ref,
    gram_ref,
    grad_query_ref,
    grad_kv_ref,
    squares_ref,
    sum_ref,
    row_dot_ref,
):
    rows = query_ref.shape[0]
    blocks = kv_ref.shape[0] // rows
    heads = groups * GROUP
    own = lax.axis_index("ctx")

    def prepare(head, _):
        attended = attended_ref[columns(head), :]
        grad_turned = grad_ref[:, columns(head)].T
        row_dot_ref[pl.ds(head, 1), :] = jnp.sum(
            attended.astype(jnp.float32) * grad_turned.astype(jnp.float32), axis=0, keepdims=True
        )
        attended_rows = attended.T
        products = dot(attended_rows, attended_rows, 1, 1) * gram_ref[rows:, :]
        squares_ref[pl.ds(heads + head, 1), :] = jnp.sum(products, axis=0, keepdims=True)
        return 0

    lax.fori_loop(0, heads, prepare, 0)

    def block(number, diagonal):
        row_at = pl.ds(pl.multiple_of(number * rows, rows), rows)

        def one_group(group, _):
            key_block = kv_ref[row_at, columns(group)]
            value_block = kv_ref[row_at, columns(groups + group)]
            key_turned = key_block.T
            key_sum = jnp.zeros((rows, HD), jnp.float32)
            value_sum = jnp.zeros((rows, HD), jnp.float32)
            for member in range(GROUP):
                head = group * GROUP + member
                one = pl.ds(head, 1)
                query = query_ref[:, columns(head)]
                grad = grad_ref[:, columns(head)]
                scores = dot(key_block, query, 1, 1)
                softmax = jnp.exp2(scores * SCALE2 - log_ref[one, :])
                if diagonal:
                    softmax = jnp.where(causal_keep(rows), softmax, 0.0)
                grad_prob = dot(value_block, grad, 1, 1)
                grad_score = (softmax * (grad_prob - row_dot_ref[one, :])).astype(jnp.bfloat16)
                value_sum = value_sum + dot(softmax.astype(jnp.bfloat16), grad, 1, 0)
                key_sum = key_sum + dot(grad_score, query, 1, 0)
                part = dot(key_turned, grad_score, 1, 0)
                if diagonal:
                    sum_ref[columns(head), :] = part
                else:
                    sum_ref[columns(head), :] += part
            grad_kv_ref[row_at, columns(group)] = (key_sum * SCALING).astype(jnp.bfloat16)
            grad_kv_ref[row_at, columns(groups + group)] = value_sum.astype(jnp.bfloat16)
            return 0

        lax.fori_loop(0, groups, one_group, 0)

    block(own, True)

    def step(number, _):
        block(number, False)
        return 0

    lax.fori_loop(0, own, step, 0)

    def clear(number, _):
        row_at = pl.ds(pl.multiple_of(number * rows, rows), rows)
        grad_kv_ref[row_at, :] = jnp.zeros((rows, 2 * groups * HD), jnp.bfloat16)
        return 0

    lax.fori_loop(own + 1, blocks, clear, 0)

    def finish(head, _):
        grad_query = (sum_ref[columns(head), :] * SCALING).T.astype(jnp.bfloat16)
        grad_query_ref[:, columns(head)] = grad_query
        products = dot(grad_query, grad_query, 1, 1) * gram_ref[:rows, :]
        squares_ref[pl.ds(head, 1), :] = jnp.sum(products, axis=0, keepdims=True)
        return 0

    lax.fori_loop(0, heads, finish, 0)


def whole_vmem(count):
    return [pl.BlockSpec(memory_space=pltpu.VMEM)] * count


def body(model, hidden_in, query_rows, key_rows, value_rows, out_weight, grad_out, answer_mask):
    rows, width = query_rows.shape
    groups = key_rows.shape[1] // HD
    heads = groups * GROUP
    loss_weight = 0.25 + answer_mask.astype(jnp.float32)
    weighted = (grad_out.astype(jnp.float32) * loss_weight[:, None]).astype(jnp.bfloat16)
    kv_all = lax.all_gather(
        jnp.concatenate([key_rows, value_rows], axis=1), "ctx", axis=0, tiled=True
    )
    piece_part = lax.all_gather(weighted, "head", axis=1, tiled=True)
    tokens = kv_all.shape[0]
    grams = jnp.concatenate(
        [dot(hidden_in, hidden_in, 1, 1), dot(weighted, weighted, 1, 1)], axis=0
    )
    grams = lax.psum(grams, "head")
    pairs = rows * tokens * heads * HD * 2
    attended, log_total = pl.pallas_call(
        functools.partial(forward_kernel, groups),
        out_shape=(
            jax.ShapeDtypeStruct((width, rows), jnp.bfloat16),
            jax.ShapeDtypeStruct((heads, rows), jnp.float32),
        ),
        in_specs=whole_vmem(2),
        out_specs=tuple(whole_vmem(2)),
        scratch_shapes=[
            pltpu.VMEM((width, rows), jnp.float32),
            pltpu.VMEM((heads, rows), jnp.float32),
            pltpu.VMEM((heads, rows), jnp.float32),
        ],
        compiler_params=pltpu.CompilerParams(vmem_limit_bytes=VMEM_LIMIT),
        cost_estimate=pl.CostEstimate(
            flops=4 * pairs, bytes_accessed=8 << 20, transcendentals=rows * tokens * heads
        ),
        name="forward",
    )(query_rows, kv_all)
    grad_attended = dot(piece_part, out_weight, 1, 1).astype(jnp.bfloat16)
    grad_query, grad_kv, squares = pl.pallas_call(
        functools.partial(backward_kernel, groups),
        out_shape=(
            jax.ShapeDtypeStruct((rows, width), jnp.bfloat16),
            jax.ShapeDtypeStruct((tokens, 2 * groups * HD), jnp.bfloat16),
            jax.ShapeDtypeStruct((2 * heads, rows), jnp.float32),
        ),
        in_specs=whole_vmem(6),
        out_specs=tuple(whole_vmem(3)),
        scratch_shapes=[
            pltpu.VMEM((width, rows), jnp.float32),
            pltpu.VMEM((heads, rows), jnp.float32),
        ],
        compiler_params=pltpu.CompilerParams(vmem_limit_bytes=VMEM_LIMIT),
        cost_estimate=pl.CostEstimate(
            flops=10 * pairs, bytes_accessed=8 << 20, transcendentals=rows * tokens * heads
        ),
        name="backward",
    )(query_rows, kv_all, grad_attended, attended, log_total, grams)
    key_sums = lax.psum_scatter(grad_kv, "ctx", scatter_dimension=0, tiled=True)
    grad_key = key_sums[:, : groups * HD]
    grad_value = key_sums[:, groups * HD :]
    normal_size = model * HD * rows
    sums = jnp.maximum(jnp.sum(squares, axis=1), 0.0)
    fisher = jnp.log(sums / normal_size + EPSILON).reshape(2, heads)
    return (grad_query, grad_key, grad_value, fisher[:1], fisher[1:])


def solution(mesh):
    spread = P("ctx", "head")

    def whole(hidden_in, *others):
        return jax.shard_map(
            functools.partial(body, hidden_in.shape[1]),
            mesh=mesh,
            in_specs=(spread, spread, spread, spread, P("head", None), spread, P("ctx")),
            out_specs=(spread,) * 5,
            check_vma=False,
        )(hidden_in, *others)

    return whole
```

time: 263 us -> 234 us (0.89)
  matrix products: 63.2 us -> 19.2 us
  Pallas kernels: 0 us -> 25.1 us
  local copies, waits for them, and re-layouts: 26.4 us -> 2.29 us
  waiting for transfers between devices: 144 us -> 167 us
  other arithmetic: 12.7 us -> 6.64 us
    dot_general x17 -> x3, matrix products: 63.2 us -> 19.2 us  [dot(): lax.dot_general(left, right, (((left_dim,), (right_dim,)), ((), ())), pre...]
    psum x0 -> x1, waiting for transfers between devices: none -> 31.7 us  [body(): grams = lax.psum(grams, 'head')]
    pallas_call x0 -> x2, Pallas kernels: none -> 25.1 us  [the longest x1 17.3 us: body(): pl.pallas_call(functools.partial(backward_kernel, groups), out_shape=(jax...]
    all_gather x3 -> x1, waiting for transfers between devices: 38.1 us -> 25.7 us  [body(): lax.all_gather(jnp.concatenate([key_rows, value_rows], axis=1), 'ctx', ax...]
    unnamed x22 -> x2, local copies, waits for them, and re-layouts: 7.31 us -> 0.01 us
    all_gather x1, waiting for transfers between devices: 40 us -> 46.9 us  [body(): piece_part = lax.all_gather(weighted, 'head', axis=1, tiled=True)]
    slice x11 -> x2, local copies, waits for them, and re-layouts: 8.29 us -> 2.28 us  [the longest x1 1.68 us: body(): grad_value = key_sums[:, groups * HD:]]
    another operation x9 -> x0, local copies, waits for them, and re-layouts: 3.93 us -> none
  transfers between devices with their start and end apart: 5 -> 4, of which waited for: 4 -> 4; matrix products, arithmetic and copies ran while one was open for 38% -> 11% of each run, Pallas kernels for 0% -> 3%
where the time goes in v1:
time: 234 us
  waiting for transfers between devices  167 us (71%)
  Pallas kernels  25.1 us (11%)
  matrix products  19.2 us (8%)
  between operations  13.8 us (6%)
  other arithmetic  6.64 us (3%)
    reduce_scatter x1, waiting for transfers between devices, body(): key_sums = lax.psum_scatter(grad_kv, 'ctx', scatter_dimension=0, tiled=True)  62.6 us
    all_gather x1, waiting for transfers between devices, body(): piece_part = lax.all_gather(weighted, 'head', axis=1, tiled=True)  46.9 us
    psum x1, waiting for transfers between devices, body(): grams = lax.psum(grams, 'head')  31.7 us
    all_gather x1, waiting for transfers between devices, body(): lax.all_gather(jnp.concatenate([key_rows, value_rows], axis=1), 'ctx', ax...  25.7 us
    dot_general x3, matrix products, dot(): lax.dot_general(left, right, (((left_dim,), (right_dim,)), ((), ())), pre...  19.2 us
    pallas_call x1, Pallas kernels, body(): pl.pallas_call(functools.partial(backward_kernel, groups), out_shape=(jax...  17.3 us
    pallas_call x1, Pallas kernels, body(): pl.pallas_call(functools.partial(forward_kernel, groups), out_shape=(jax....  7.77 us
  transfers between devices with their start and end apart: 4, of which 4 were waited for; matrix products, arithmetic and copies ran while one was open for 11% of the time, Pallas kernels for 3%

profile of v1, /device:TPU:0, one launch (start us, length us, event | category | flops | bytes accessed | tf_op | source)
XLA Modules:
  0.0 234.1 jit_solution(7082827817283243777)
XLA Ops:
  7.2 0.0 copy-start
  7.2 0.0 all-gather.3.cloned.1.call-start
  7.2 1.8 pad_maximum_fusion.1
  9.0 0.0 all-gather.3.cloned.1.call-update
  9.0 0.0 all-gather.5.cloned.1.call-start
  9.1 0.7 convert_add_fusion
  9.7 2.4 %multiply_convert_fusion = bf16[256,2048]{1,0:T(8,128)(2,1)} fusion(bf16[256,2048]{1,0:T(8,128)(2,1)} %param.12, f32[256]{0:T(256)S(1)} %convert_add_fusion), kind=kLoop, calls=%fused_computation.1 | loop fusion | flops 1572864 | bytes 2098176 | tf_op jit(solution)/shard_map/convert_element_type | solution.py:184
  12.2 0.0 all-gather.5.cloned.1.call-update
  12.2 0.0 all-reduce.2.cloned.1.call-start
  12.3 2.0 fusion.2
  14.3 0.0 copy-done
  14.3 0.5 fusion.1
  14.8 0.9 pad_maximum_fusion
  15.6 0.0 all-reduce.2.cloned.1.call-update
  15.7 0.0 reduce-scatter.2.cloned.1.call-start
  15.7 25.7 %all-gather.3.cloned.1.call-done.kv_ref = bf16[2048,512]{1,0:T(8,128)(2,1)} async-done(((bf16[256,512]{1,0:T(8,128)(2,1)}), bf16[2048,512]{1,0:T(8,128)(2,1)}) %all-gather.3.cloned.1.call-update) | async-done | bytes 2097168 | tf_op jit(solution)/shard_map/all_gather | solution.py:185
  41.5 7.8 %forward.1 = (bf16[2048,256]{1,0:T(8,128)(2,1)}, f32[16,256]{1,0:T(8,128)}) custom-call(bf16[256,2048]{1,0:T(8,128)(2,1)} %query_ref.3, bf16[2048,512]{1,0:T(8,128)(2,1)} %all-gather.3.cloned.1.call-done.kv_ref), custom_call_target="tpu_custom_call" | custom-call | flops 8589934592 | bytes 8388608 | tf_op jit(solution)/shard_map/forward/pallas_call | solution.py:195
  49.2 46.9 %all-gather.5.cloned.1.call-done = bf16[256,8192]{1,0:T(8,128)(2,1)} async-done(((bf16[256,2048]{1,0:T(8,128)(2,1)}), bf16[256,8192]{1,0:T(8,128)(2,1)}) %all-gather.5.cloned.1.call-update) | async-done | bytes 4194320 | tf_op jit(solution)/shard_map/all_gather | solution.py:188
  96.1 16.7 %convolution_convert_fusion.grad_ref = bf16[256,2048]{1,0:T(8,128)(2,1)} fusion(bf16[256,8192]{1,0:T(8,128)(2,1)} %all-gather.5.cloned.1.call-done, bf16[2048,8192]{1,0:T(8,128)(2,1)} %param.11), kind=kOutput, calls=%fused_computation | convolution fusion | flops 8590458880 | bytes 38797312 | tf_op jit(solution)/shard_map/dot_general | solution.py:21
  112.8 31.7 %all-reduce.2.cloned.1.call-done.gram_ref = f32[512,256]{1,0:T(8,128)} async-done(((f32[512,256]{1,0:T(8,128)}), f32[512,256]{1,0:T(8,128)}) %all-reduce.2.cloned.1.call-update) | async-done | bytes 524304 | tf_op jit(solution)/shard_map/psum | solution.py:193
  144.5 17.3 %backward.1 = (bf16[256,2048]{1,0:T(8,128)(2,1)}, bf16[2048,512]{1,0:T(8,128)(2,1)}, f32[32,256]{1,0:T(8,128)}) custom-call(bf16[256,2048]{1,0:T(8,128)(2,1)} %query_ref.3, bf16[2048,512]{1,0:T(8,128)(2,1)} %all-gather.3.cloned.1.call-done.kv_ref, bf16[256,2048]{1,0:T(8,128)(2,1)} %convolution_convert_fusion.grad_ref, ...), custom_call_target="tpu_custom_call" | custom-call | flops 21474836480 | bytes 8388608 | tf_op jit(solution)/shard_map/backward/pallas_call | solution.py:215
  161.8 0.0 reduce-scatter.2.cloned.1.call-update
  161.8 0.9 reduce_sum.9
  162.7 0.6 slice_bitcast_fusion
  163.3 62.6 %reduce-scatter.2.cloned.1.call-done = bf16[256,512]{1,0:T(8,128)(2,1)} async-done(((bf16[2048,512]{1,0:T(8,128)(2,1)}), bf16[256,512]{1,0:T(8,128)(2,1)}) %reduce-scatter.2.cloned.1.call-update) | async-done | bytes 262160 | tf_op jit(solution)/shard_map/reduce_scatter | solution.py:234
  225.9 1.7 fusion
  (1 shorter events, 0.0 us)
Async XLA Ops:
  7.2 7.1 %copy-start = (bf16[256,2048]{1,0:T(8,128)(2,1)S(1)}, bf16[256,2048]{1,0:T(8,128)(2,1)}, u32[]{:S(2)}) copy-start(bf16[256,2048]{1,0:T(8,128)(2,1)} %param.7) | copy-start | bytes 3145732
  7.2 34.3 %all-gather.3.cloned.1.call-start = ((), (), s32[]{:S(2)}) async-start(), calls=%async_computation.1 | async-start | bytes 2359296 | tf_op jit(solution)/shard_map/all_gather | solution.py:185
  9.0 87.1 %all-gather.5.cloned.1.call-start = ((), (), s32[]{:S(2)}) async-start(), calls=%async_computation.2 | async-start | bytes 5242880 | tf_op jit(solution)/shard_map/all_gather | solution.py:188
  12.2 132.3 %all-reduce.2.cloned.1.call-start = ((), (), s32[]{:S(2)}) async-start(), calls=%async_computation.3 | async-start | bytes 1048576 | tf_op jit(solution)/shard_map/psum | solution.py:193
  15.7 210.2 %reduce-scatter.2.cloned.1.call-start = ((), (), s32[]{:S(2)}) async-start(), calls=%async_computation.4 | async-start | bytes 2359296 | tf_op jit(solution)/shard_map/reduce_scatter | solution.py:234
Sparse Core Ops, SparseCore 0:
  9.6 31.7 all-gather.2
  43.9 52.1 all-gather.4
  99.1 45.3 all-reduce.1
  161.9 63.8 reduce-scatter.1

commit v2 on v1

v2 whole, which is shorter than its diff:
```python
import functools

import jax
import jax.numpy as jnp
from jax import lax
from jax.experimental import pallas as pl
from jax.experimental.pallas import tpu as pltpu
from jax.sharding import PartitionSpec as P

HD = 128
GROUP = 8
NEGATIVE = -1e30
EPSILON = 1e-06
SCALING = HD ** (-0.5)
LOG2E = 1.4426950408889634
SCALE2 = SCALING * LOG2E
VMEM_LIMIT = 56 * 1024 * 1024


def dot(left, right, left_dim, right_dim):
    return lax.dot_general(
        left, right, (((left_dim,), (right_dim,)), ((), ())), preferred_element_type=jnp.float32
    )


def columns(index):
    if isinstance(index, int):
        return slice(index * HD, (index + 1) * HD)
    return pl.ds(pl.multiple_of(index * HD, HD), HD)


def causal_keep(rows):
    key_pos = lax.broadcasted_iota(jnp.int32, (rows, rows), 0)
    query_pos = lax.broadcasted_iota(jnp.int32, (rows, rows), 1)
    return key_pos <= query_pos


def forward_kernel(groups, query_ref, kv_ref, attended_ref, log_ref, sum_ref, max_ref, total_ref):
    rows = query_ref.shape[0]
    own = lax.axis_index("ctx")

    def block(number, diagonal):
        row_at = pl.ds(pl.multiple_of(number * rows, rows), rows)

        for group in range(groups):
            key_block = kv_ref[row_at, columns(group)]
            value_turned = kv_ref[row_at, columns(groups + group)].T
            for member in range(GROUP):
                head = group * GROUP + member
                scores = dot(key_block, query_ref[:, columns(head)], 1, 1)
                one = slice(head, head + 1)
                if diagonal:
                    scores = jnp.where(causal_keep(rows), scores, NEGATIVE)
                    new_max = jnp.max(scores, axis=0, keepdims=True)
                else:
                    old_max = max_ref[one, :]
                    new_max = jnp.maximum(old_max, jnp.max(scores, axis=0, keepdims=True))
                weights = jnp.exp2(scores * SCALE2 - new_max * SCALE2)
                weights_sum = jnp.sum(weights, axis=0, keepdims=True)
                part = dot(value_turned, weights.astype(jnp.bfloat16), 1, 0)
                if diagonal:
                    total_ref[one, :] = weights_sum
                    sum_ref[columns(head), :] = part
                else:
                    factor = jnp.exp2((old_max - new_max) * SCALE2)
                    total_ref[one, :] = total_ref[one, :] * factor + weights_sum
                    sum_ref[columns(head), :] = sum_ref[columns(head), :] * factor + part
                max_ref[one, :] = new_max

    block(own, True)

    def step(number, _):
        block(number, False)
        return 0

    lax.fori_loop(0, own, step, 0)
    for head in range(groups * GROUP):
        total = total_ref[head : head + 1, :]
        log_ref[head : head + 1, :] = max_ref[head : head + 1, :] * SCALE2 + jnp.log2(total)
        part = sum_ref[head * HD : (head + 1) * HD, :]
        attended_ref[head * HD : (head + 1) * HD, :] = (part / total).astype(jnp.bfloat16)


def backward_kernel(
    groups,
    group,
    query_ref,
    kv_ref,
    grad_ref,
    attended_ref,
    log_ref,
    grad_query_ref,
    grad_kv_ref,
    sum_ref,
    row_dot_ref,
):
    rows = query_ref.shape[0]
    blocks = kv_ref.shape[0] // rows
    own = lax.axis_index("ctx")
    for member in range(GROUP):
        head = group * GROUP + member
        attended = attended_ref[columns(head), :]
        grad_turned = grad_ref[:, columns(head)].T
        row_dot_ref[member : member + 1, :] = jnp.sum(
            attended.astype(jnp.float32) * grad_turned.astype(jnp.float32), axis=0, keepdims=True
        )

    def block(number, diagonal):
        row_at = pl.ds(pl.multiple_of(number * rows, rows), rows)

        key_block = kv_ref[row_at, columns(group)]
        value_block = kv_ref[row_at, columns(groups + group)]
        key_turned = key_block.T
        key_sum = jnp.zeros((rows, HD), jnp.float32)
        value_sum = jnp.zeros((rows, HD), jnp.float32)
        for member in range(GROUP):
            head = group * GROUP + member
            query = query_ref[:, columns(head)]
            grad = grad_ref[:, columns(head)]
            scores = dot(key_block, query, 1, 1)
            softmax = jnp.exp2(scores * SCALE2 - log_ref[head : head + 1, :])
            if diagonal:
                softmax = jnp.where(causal_keep(rows), softmax, 0.0)
            grad_prob = dot(value_block, grad, 1, 1)
            row_dot = row_dot_ref[member : member + 1, :]
            grad_score = (softmax * (grad_prob - row_dot)).astype(jnp.bfloat16)
            value_sum = value_sum + dot(softmax.astype(jnp.bfloat16), grad, 1, 0)
            key_sum = key_sum + dot(grad_score, query, 1, 0)
            part = dot(key_turned, grad_score, 1, 0)
            if diagonal:
                sum_ref[columns(member), :] = part
            else:
                sum_ref[columns(member), :] += part
        grad_kv_ref[row_at, :HD] = (key_sum * SCALING).astype(jnp.bfloat16)
        grad_kv_ref[row_at, HD:] = value_sum.astype(jnp.bfloat16)

    block(own, True)

    def step(number, _):
        block(number, False)
        return 0

    lax.fori_loop(0, own, step, 0)

    def clear(number, _):
        row_at = pl.ds(pl.multiple_of(number * rows, rows), rows)
        grad_kv_ref[row_at, :] = jnp.zeros((rows, 2 * HD), jnp.bfloat16)
        return 0

    lax.fori_loop(own + 1, blocks, clear, 0)

    for member in range(GROUP):
        grad_query = (sum_ref[columns(member), :] * SCALING).T.astype(jnp.bfloat16)
        grad_query_ref[:, columns(member)] = grad_query


def squares_kernel(heads, grad_query_ref, attended_ref, gram_ref, squares_ref):
    rows = grad_query_ref.shape[0]

    def one_head(head, _):
        grad_query = grad_query_ref[:, columns(head)]
        products = dot(grad_query, grad_query, 1, 1) * gram_ref[:rows, :]
        squares_ref[pl.ds(head, 1), :] = jnp.sum(products, axis=0, keepdims=True)
        attended = attended_ref[columns(head), :].T
        products = dot(attended, attended, 1, 1) * gram_ref[rows:, :]
        squares_ref[pl.ds(heads + head, 1), :] = jnp.sum(products, axis=0, keepdims=True)
        return 0

    lax.fori_loop(0, heads, one_head, 0)


def whole_vmem(count):
    return [pl.BlockSpec(memory_space=pltpu.VMEM)] * count


def body(model, hidden_in, query_rows, key_rows, value_rows, out_weight, grad_out, answer_mask):
    rows, width = query_rows.shape
    groups = key_rows.shape[1] // HD
    heads = groups * GROUP
    loss_weight = 0.25 + answer_mask.astype(jnp.float32)
    weighted = (grad_out.astype(jnp.float32) * loss_weight[:, None]).astype(jnp.bfloat16)
    kv_all = lax.all_gather(
        jnp.concatenate([key_rows, value_rows], axis=1), "ctx", axis=0, tiled=True
    )
    own_head = lax.axis_index("head")
    head_devices = model // width
    piece_part = jnp.zeros((rows, model), jnp.bfloat16)
    pieces = [weighted] + [
        lax.ppermute(weighted, "head", [(at, at ^ far) for at in range(head_devices)])
        for far in range(1, head_devices)
    ]
    tokens = kv_all.shape[0]
    grams = jnp.concatenate(
        [dot(hidden_in, hidden_in, 1, 1), dot(weighted, weighted, 1, 1)], axis=0
    )
    pairs = rows * tokens * heads * HD * 2
    attended, log_total = pl.pallas_call(
        functools.partial(forward_kernel, groups),
        out_shape=(
            jax.ShapeDtypeStruct((width, rows), jnp.bfloat16),
            jax.ShapeDtypeStruct((heads, rows), jnp.float32),
        ),
        in_specs=whole_vmem(2),
        out_specs=tuple(whole_vmem(2)),
        scratch_shapes=[
            pltpu.VMEM((width, rows), jnp.float32),
            pltpu.VMEM((heads, rows), jnp.float32),
            pltpu.VMEM((heads, rows), jnp.float32),
        ],
        compiler_params=pltpu.CompilerParams(vmem_limit_bytes=VMEM_LIMIT),
        cost_estimate=pl.CostEstimate(
            flops=4 * pairs, bytes_accessed=8 << 20, transcendentals=rows * tokens * heads
        ),
        name="forward",
    )(query_rows, kv_all)
    grams, attended = lax.optimization_barrier((grams, attended))
    grams = lax.psum(grams, "head")
    attended, *pieces = lax.optimization_barrier((attended, *pieces))
    for far, piece in enumerate(pieces):
        piece_part = lax.dynamic_update_slice(piece_part, piece, (0, (own_head ^ far) * width))
    grad_attended = dot(piece_part, out_weight, 1, 1).astype(jnp.bfloat16)
    query_grads, key_grads, value_grads = [], [], []
    for group in range(groups):
        grad_part, grad_kv = pl.pallas_call(
            functools.partial(backward_kernel, groups, group),
            out_shape=(
                jax.ShapeDtypeStruct((rows, GROUP * HD), jnp.bfloat16),
                jax.ShapeDtypeStruct((tokens, 2 * HD), jnp.bfloat16),
            ),
            in_specs=whole_vmem(5),
            out_specs=tuple(whole_vmem(2)),
            scratch_shapes=[
                pltpu.VMEM((GROUP * HD, rows), jnp.float32),
                pltpu.VMEM((GROUP, rows), jnp.float32),
            ],
            compiler_params=pltpu.CompilerParams(vmem_limit_bytes=VMEM_LIMIT),
            cost_estimate=pl.CostEstimate(
                flops=10 * pairs // groups,
                bytes_accessed=8 << 20,
                transcendentals=rows * tokens * GROUP,
            ),
            name="backward",
        )(query_rows, kv_all, grad_attended, attended, log_total)
        key_sums = lax.psum_scatter(grad_kv, "ctx", scatter_dimension=0, tiled=True)
        query_grads.append(grad_part)
        key_grads.append(key_sums[:, :HD])
        value_grads.append(key_sums[:, HD:])
    grad_query = jnp.concatenate(query_grads, axis=1)
    grad_key = jnp.concatenate(key_grads, axis=1)
    grad_value = jnp.concatenate(value_grads, axis=1)
    squares = pl.pallas_call(
        functools.partial(squares_kernel, heads),
        out_shape=jax.ShapeDtypeStruct((2 * heads, rows), jnp.float32),
        in_specs=whole_vmem(3),
        out_specs=whole_vmem(1)[0],
        compiler_params=pltpu.CompilerParams(vmem_limit_bytes=VMEM_LIMIT),
        name="squares",
    )(grad_query, attended, grams)
    normal_size = model * HD * rows
    sums = jnp.maximum(jnp.sum(squares, axis=1), 0.0)
    fisher = jnp.log(sums / normal_size + EPSILON).reshape(2, heads)
    return (grad_query, grad_key, grad_value, fisher[:1], fisher[1:])


def solution(mesh):
    spread = P("ctx", "head")

    def whole(hidden_in, *others):
        return jax.shard_map(
            functools.partial(body, hidden_in.shape[1]),
            mesh=mesh,
            in_specs=(spread, spread, spread, spread, P("head", None), spread, P("ctx")),
            out_specs=(spread,) * 5,
            check_vma=False,
        )(hidden_in, *others)

    return whole
```

time: 234 us -> 204 us (0.87)
  waiting for transfers between devices: 167 us -> 120 us
  local copies, waits for them, and re-layouts: 2.29 us -> 12.7 us
  starting transfers between devices: 0.16 us -> 4.89 us
    all_gather x1 -> x0, waiting for transfers between devices: 46.9 us -> none  [body(): piece_part = lax.all_gather(weighted, 'head', axis=1, tiled=True)]
    ppermute x0 -> x3, waiting for transfers between devices: none -> 11.8 us  [body(): lax.ppermute(weighted, 'head', [(at, at ^ far) for at in range(head_devic...]
    dynamic_update_slice x0 -> x4, local copies, waits for them, and re-layouts: none -> 6.79 us  [body(): lax.dynamic_update_slice(piece_part, piece, (0, (own_head ^ far) * width))]
    ppermute x0 -> x3, starting transfers between devices: none -> 4.54 us  [body(): lax.ppermute(weighted, 'head', [(at, at ^ far) for at in range(head_devic...]
    reduce_scatter x1 -> x2, waiting for transfers between devices: 62.6 us -> 58.2 us  [body(): key_sums = lax.psum_scatter(grad_kv, 'ctx', scatter_dimension=0, tiled=True)]
    psum x1, waiting for transfers between devices: 31.7 us -> 27.6 us  [body(): grams = lax.psum(grams, 'head')]
    all_gather x1, waiting for transfers between devices: 25.7 us -> 22.8 us  [body(): lax.all_gather(jnp.concatenate([key_rows, value_rows], axis=1), 'ctx', ax...]
    broadcast_in_dim x0 -> x1, local copies, waits for them, and re-layouts: none -> 2.42 us  [body(): piece_part = jnp.zeros((rows, model), jnp.bfloat16)]
  transfers between devices with their start and end apart: 4 -> 7, of which waited for: 4 -> 5; matrix products, arithmetic and copies ran while one was open for 11% -> 17% of each run, Pallas kernels for 3% -> 13%
where the time goes in v2:
time: 204 us
  waiting for transfers between devices  120 us (59%)
  Pallas kernels  26.2 us (13%)
  matrix products  18.3 us (9%)
  between operations  13.8 us (7%)
  local copies, waits for them, and re-layouts  12.7 us (6%)
  other arithmetic  7.31 us (4%)
  starting transfers between devices  4.89 us (2%)
    reduce_scatter x2, waiting for transfers between devices, body(): key_sums = lax.psum_scatter(grad_kv, 'ctx', scatter_dimension=0, tiled=True)  58.2 us
    psum x1, waiting for transfers between devices, body(): grams = lax.psum(grams, 'head')  27.6 us
    all_gather x1, waiting for transfers between devices, body(): lax.all_gather(jnp.concatenate([key_rows, value_rows], axis=1), 'ctx', ax...  22.8 us
    dot_general x3, matrix products, dot(): lax.dot_general(left, right, (((left_dim,), (right_dim,)), ((), ())), pre...  18.3 us
    ppermute x3, waiting for transfers between devices, body(): lax.ppermute(weighted, 'head', [(at, at ^ far) for at in range(head_devic...  11.8 us
    pallas_call x2, Pallas kernels, body(): pl.pallas_call(functools.partial(backward_kernel, groups, group), out_sha...  11.7 us
    pallas_call x1, Pallas kernels, body(): pl.pallas_call(functools.partial(forward_kernel, groups), out_shape=(jax....  7.58 us
    pallas_call x1, Pallas kernels, body(): pl.pallas_call(functools.partial(squares_kernel, heads), out_shape=jax.Sh...  6.85 us
  transfers between devices with their start and end apart: 7, of which 5 were waited for; matrix products, arithmetic and copies ran while one was open for 17% of the time, Pallas kernels for 13%

profile of v2, /device:TPU:0, one launch (start us, length us, event | category | flops | bytes accessed | tf_op | source)
XLA Modules:
  0.0 203.7 jit_solution(1985621405934316796)
XLA Ops:
  7.2 1.8 pad_maximum_fusion.1
  9.0 0.0 all-reduce.2.cloned.1.call-start
  9.1 0.7 convert_add_fusion
  9.8 1.5 multiply_convert_fusion
  11.2 3.0 %collective-permute-start = (bf16[256,2048]{1,0:T(8,128)(2,1)S(1)}, bf16[256,2048]{1,0:T(8,128)(2,1)S(1)}, u32[]{:S(2)}, u32[]{:S(2)}) collective-permute-start(bf16[256,2048]{1,0:T(8,128)(2,1)S(1)} %multiply_convert_fusion), channel_id=1, source_target_pairs={{0,1},{1,0},{2,3},{3,2},{4,5},{5,4},{6,7},{7,6},{8,9},{9,8},{10,11... | collective-permute-start | bytes 3145736 | tf_op jit(solution)/shard_map/ppermute | solution.py:189
  14.2 1.5 collective-permute-start.1
  15.8 0.5 fusion.3
  16.3 1.2 fusion.2
  17.4 1.8 pad_maximum_fusion
  19.2 22.8 %all-gather.2.cloned.1.call-done.kv_ref = bf16[2048,512]{1,0:T(8,128)(2,1)} async-done(((bf16[256,512]{1,0:T(8,128)(2,1)}), bf16[2048,512]{1,0:T(8,128)(2,1)}) %all-gather.2.cloned.1.call-update) | async-done | bytes 2097168 | tf_op jit(solution)/shard_map/all_gather | solution.py:182
  42.0 7.6 %forward.1 = (bf16[2048,256]{1,0:T(8,128)(2,1)}, f32[16,256]{1,0:T(8,128)}) custom-call(bf16[256,2048]{1,0:T(8,128)(2,1)} %query_ref.5, bf16[2048,512]{1,0:T(8,128)(2,1)} %all-gather.2.cloned.1.call-done.kv_ref), custom_call_target="tpu_custom_call" | custom-call | flops 8589934592 | bytes 8388608 | tf_op jit(solution)/shard_map/forward/pallas_call | solution.py:197
  49.6 11.8 %collective-permute-done.1 = bf16[256,2048]{1,0:T(8,128)(2,1)} collective-permute-done((bf16[256,2048]{1,0:T(8,128)(2,1)S(1)}, bf16[256,2048]{1,0:T(8,128)(2,1)}, u32[]{:S(2)}, u32[]{:S(2)}) %collective-permute-start.1) | collective-permute-done | bytes 1048608 | tf_op jit(solution)/shard_map/ppermute | solution.py:189
  61.4 0.2 reduce-scatter.5.cloned.1.call-start
  61.7 2.4 %broadcast_in_dim.4 = bf16[256,8192]{1,0:T(8,128)(2,1)} broadcast(bf16[]{:T(256)} %constant.12.clone.1), dimensions={} | broadcast | bytes 4194306 | tf_op jit(solution)/shard_map/broadcast_in_dim | solution.py:187
  64.1 1.0 constant_dynamic-update-slice_fusion.5
  65.1 1.0 constant_dynamic-update-slice_fusion.4
  66.2 2.3 %constant_dynamic-update-slice_fusion.3 = bf16[256,8192]{1,0:T(8,128)(2,1)} fusion(bf16[256,8192]{1,0:T(8,128)(2,1)} %constant_dynamic-update-slice_fusion.4, bf16[256,2048]{1,0:T(8,128)(2,1)} %collective-permute-done.1, s32[]{:T(128)S(6)} %select_n.14), kind=kLoop, calls=%fused_computation.9 | loop fusion | bytes 2097156 | tf_op jit(solution)/shard_map/dynamic_update_slice | solution.py:220
  68.5 2.4 %constant_dynamic-update-slice_fusion.2 = bf16[256,8192]{1,0:T(8,128)(2,1)} fusion(bf16[256,8192]{1,0:T(8,128)(2,1)} %constant_dynamic-update-slice_fusion.3, bf16[256,2048]{1,0:T(8,128)(2,1)} %collective-permute-done.2, s32[]{:T(128)S(6)} %select_n.15), kind=kLoop, calls=%fused_computation.8 | loop fusion | bytes 2097156 | tf_op jit(solution)/shard_map/dynamic_update_slice | solution.py:220
  70.9 16.6 %convolution_convert_fusion.grad_ref = bf16[256,2048]{1,0:T(8,128)(2,1)} fusion(bf16[256,8192]{1,0:T(8,128)(2,1)} %constant_dynamic-update-slice_fusion.2, bf16[2048,8192]{1,0:T(8,128)(2,1)} %param.11), kind=kOutput, calls=%fused_computation | convolution fusion | flops 8590458880 | bytes 38797312 | tf_op jit(solution)/shard_map/dot_general | solution.py:21
  87.5 5.9 %backward.3 = (bf16[256,1024]{1,0:T(8,128)(2,1)}, bf16[2048,256]{1,0:T(8,128)(2,1)}) custom-call(bf16[256,2048]{1,0:T(8,128)(2,1)} %query_ref.5, bf16[2048,512]{1,0:T(8,128)(2,1)} %all-gather.2.cloned.1.call-done.kv_ref, bf16[256,2048]{1,0:T(8,128)(2,1)} %convolution_convert_fusion.grad_ref, bf16[2048,256]{1,0:T(8,128)(2,1)} %get-tuple-element.24.attended_ref, ...), custom_call_target="tpu_custom_call" | custom-call | flops 10737418240 | bytes 8388608 | tf_op jit(solution)/shard_map/backward/pallas_call | solution.py:224
  93.4 0.0 reduce-scatter.3.cloned.1.call-start
  93.5 5.9 %backward.2 = (bf16[256,1024]{1,0:T(8,128)(2,1)}, bf16[2048,256]{1,0:T(8,128)(2,1)}) custom-call(bf16[256,2048]{1,0:T(8,128)(2,1)} %query_ref.5, bf16[2048,512]{1,0:T(8,128)(2,1)} %all-gather.2.cloned.1.call-done.kv_ref, bf16[256,2048]{1,0:T(8,128)(2,1)} %convolution_convert_fusion.grad_ref, bf16[2048,256]{1,0:T(8,128)(2,1)} %get-tuple-element.24.attended_ref, ...), custom_call_target="tpu_custom_call" | custom-call | flops 10737418240 | bytes 8388608 | tf_op jit(solution)/shard_map/backward/pallas_call | solution.py:224
  99.4 1.1 constant_dynamic-update-slice_fusion.1
  100.5 27.6 %all-reduce.2.cloned.1.call-done.gram_ref = f32[512,256]{1,0:T(8,128)} async-done(((f32[512,256]{1,0:T(8,128)}), f32[512,256]{1,0:T(8,128)}) %all-reduce.2.cloned.1.call-update) | async-done | bytes 524304 | tf_op jit(solution)/shard_map/psum | solution.py:217
  128.1 6.8 %squares.1 = f32[32,256]{1,0:T(8,128)} custom-call(bf16[256,2048]{1,0:T(8,128)(2,1)} %copy-done.1, bf16[2048,256]{1,0:T(8,128)(2,1)} %get-tuple-element.24.attended_ref, f32[512,256]{1,0:T(8,128)} %all-reduce.2.cloned.1.call-done.gram_ref), custom_call_target="tpu_custom_call" | custom-call | tf_op jit(solution)/shard_map/squares/pallas_call | solution.py:251
  134.9 0.9 reduce_sum.9
  135.8 0.6 slice_bitcast_fusion
  136.4 26.4 %reduce-scatter.5.cloned.1.call-done = bf16[256,256]{1,0:T(8,128)(2,1)} async-done(((bf16[2048,256]{1,0:T(8,128)(2,1)}), bf16[256,256]{1,0:T(8,128)(2,1)}) %reduce-scatter.5.cloned.1.call-update) | async-done | bytes 131088 | tf_op jit(solution)/shard_map/reduce_scatter | solution.py:244
  162.8 0.9 fusion.1
  163.6 31.9 %reduce-scatter.3.cloned.1.call-done = bf16[256,256]{1,0:T(8,128)(2,1)} async-done(((bf16[2048,256]{1,0:T(8,128)(2,1)}), bf16[256,256]{1,0:T(8,128)(2,1)}) %reduce-scatter.3.cloned.1.call-update) | async-done | bytes 131088 | tf_op jit(solution)/shard_map/reduce_scatter | solution.py:244
  195.5 0.9 fusion
  196.4 0.7 pad_maximum_fusion.2
  (16 shorter events, 0.2 us)
Async XLA Ops:
  7.2 9.1 %copy-start = (bf16[256,2048]{1,0:T(8,128)(2,1)S(1)}, bf16[256,2048]{1,0:T(8,128)(2,1)}, u32[]{:S(2)}) copy-start(bf16[256,2048]{1,0:T(8,128)(2,1)} %param.7) | copy-start | bytes 3145732
  7.2 34.8 %all-gather.2.cloned.1.call-start = ((), (), s32[]{:S(2)}) async-start(), calls=%async_computation.2 | async-start | bytes 2359296 | tf_op jit(solution)/shard_map/all_gather | solution.py:182
  9.0 119.1 %all-reduce.2.cloned.1.call-start = ((), (), s32[]{:S(2)}) async-start(), calls=%async_computation.5 | async-start | bytes 1048576 | tf_op jit(solution)/shard_map/psum | solution.py:217
  11.2 38.4 %collective-permute-start = (bf16[256,2048]{1,0:T(8,128)(2,1)S(1)}, bf16[256,2048]{1,0:T(8,128)(2,1)S(1)}, u32[]{:S(2)}, u32[]{:S(2)}) collective-permute-start(bf16[256,2048]{1,0:T(8,128)(2,1)S(1)} %multiply_convert_fusion), channel_id=1, source_target_pairs={{0,1},{1,0},{2,3},{3,2},{4,5},{5,4},{6,7},{7,6},{8,9},{9,8},{10,11... | collective-permute-start | bytes 3145736 | tf_op jit(solution)/shard_map/ppermute | solution.py:189
  14.2 47.2 %collective-permute-start.1 = (bf16[256,2048]{1,0:T(8,128)(2,1)S(1)}, bf16[256,2048]{1,0:T(8,128)(2,1)}, u32[]{:S(2)}, u32[]{:S(2)}) collective-permute-start(bf16[256,2048]{1,0:T(8,128)(2,1)S(1)} %multiply_convert_fusion), channel_id=1, source_target_pairs={{0,2},{1,3},{2,0},{3,1},{4,6},{5,7},{6,4},{7,5},{8,10},{9,11},{10,... | collective-permute-start | bytes 3145736 | tf_op jit(solution)/shard_map/ppermute | solution.py:189
  15.7 45.7 %collective-permute-start.2 = (bf16[256,2048]{1,0:T(8,128)(2,1)S(1)}, bf16[256,2048]{1,0:T(8,128)(2,1)}, u32[]{:S(2)}, u32[]{:S(2)}) collective-permute-start(bf16[256,2048]{1,0:T(8,128)(2,1)S(1)} %multiply_convert_fusion), channel_id=1, source_target_pairs={{0,3},{1,2},{2,1},{3,0},{4,7},{5,6},{6,5},{7,4},{8,11},{9,10},{10,... | collective-permute-start | bytes 3145736 | tf_op jit(solution)/shard_map/ppermute | solution.py:189
  61.4 101.3 %reduce-scatter.5.cloned.1.call-start = ((), (), s32[]{:S(2)}) async-start(), calls=%async_computation.4 | async-start | bytes 1179648 | tf_op jit(solution)/shard_map/reduce_scatter | solution.py:244
  93.4 7.1 %copy-start.2 = (bf16[256,1024]{1,0:T(8,128)(2,1)S(1)}, bf16[256,1024]{1,0:T(8,128)(2,1)}, u32[]{:S(2)}) copy-start(bf16[256,1024]{1,0:T(8,128)(2,1)} %get-tuple-element.27) | copy-start | bytes 1572868
  93.4 102.1 %reduce-scatter.3.cloned.1.call-start = ((), (), s32[]{:S(2)}) async-start(), calls=%async_computation.3 | async-start | bytes 1179648 | tf_op jit(solution)/shard_map/reduce_scatter | solution.py:244
  100.5 27.6 %copy-start.1 = (bf16[256,2048]{1,0:T(8,128)(2,1)}, bf16[256,2048]{1,0:T(8,128)(2,1)S(1)}, u32[]{:S(2)}) copy-start(bf16[256,2048]{1,0:T(8,128)(2,1)S(1)} %constant_dynamic-update-slice_fusion.grad_query_ref) | copy-start | bytes 3145732
Sparse Core Ops, SparseCore 0:
  10.2 31.7 all-gather.1
  61.6 66.4 all-reduce.1
  130.4 32.3 reduce-scatter.4
  164.9 30.5 reduce-scatter.2

commit v3 on v2

--- a/solution.py
+++ b/solution.py
@@ -173,6 +173,67 @@
     return [pl.BlockSpec(memory_space=pltpu.VMEM)] * count
 
 
+def project_kernel(own_ref, *refs):
+    *piece_refs, weight_ref, out_ref, sum_ref = refs
+    far = pl.program_id(0)
+    tile = weight_ref.shape[0]
+    at = pl.ds(pl.multiple_of(pl.program_id(1) * tile, tile), tile)
+    for number, piece_ref in enumerate(piece_refs):
+
+        @pl.when(far == number)
+        def _():
+            total = dot(piece_ref[...], weight_ref[...], 1, 1)
+            if number:
+                total = total + sum_ref[:, at]
+            if number < len(piece_refs) - 1:
+                sum_ref[:, at] = total
+            else:
+                out_ref[:, at] = total.astype(jnp.bfloat16)
+
+
+def project(own_head, pieces, out_weight):
+    rows, width = pieces[0].shape
+    outs = out_weight.shape[0]
+    tile = 512
+    whole = pl.BlockSpec((rows, width), lambda far, at, own: (0, 0))
+    return pl.pallas_call(
+        project_kernel,
+        out_shape=jax.ShapeDtypeStruct((rows, outs), jnp.bfloat16),
+        grid_spec=pltpu.PrefetchScalarGridSpec(
+            num_scalar_prefetch=1,
+            grid=(len(pieces), outs // tile),
+            in_specs=[whole] * len(pieces)
+            + [pl.BlockSpec((tile, width), lambda far, at, own: (at, own[0] ^ far))],
+            out_specs=pl.BlockSpec((rows, outs), lambda far, at, own: (0, 0)),
+            scratch_shapes=[pltpu.VMEM((rows, outs), jnp.float32)],
+        ),
+        compiler_params=pltpu.CompilerParams(vmem_limit_bytes=VMEM_LIMIT),
+        name="project",
+    )(jnp.reshape(own_head, (1,)).astype(jnp.int32), *pieces, out_weight)
+
+
+def owner_sums(parts, rows):
+    count = parts.shape[0] // rows
+    own = lax.axis_index("ctx")
+    core, chip = own % 2, own // 2
+    blocks = parts.reshape(count // 2, 2, rows, parts.shape[1])
+
+    def of_core(index):
+        return lax.dynamic_index_in_dim(blocks, index, 1, keepdims=False)
+
+    def swapped(value, far):
+        return lax.ppermute(value, "ctx", [(at, at ^ far) for at in range(count)])
+
+    got = swapped(of_core(1 - core), 1)
+    pair = of_core(core).astype(jnp.float32) + got.astype(jnp.float32)
+    pair = pair.astype(jnp.bfloat16)
+    total = lax.dynamic_index_in_dim(pair, chip, 0, keepdims=False).astype(jnp.float32)
+    for far in range(1, count // 2):
+        piece = lax.dynamic_index_in_dim(pair, chip ^ far, 0, keepdims=False)
+        total = total + swapped(piece, 2 * far).astype(jnp.float32)
+    return total.astype(jnp.bfloat16)
+
+
 def body(model, hidden_in, query_rows, key_rows, value_rows, out_weight, grad_out, answer_mask):
     rows, width = query_rows.shape
     groups = key_rows.shape[1] // HD
@@ -184,7 +245,6 @@
     )
     own_head = lax.axis_index("head")
     head_devices = model // width
-    piece_part = jnp.zeros((rows, model), jnp.bfloat16)
     pieces = [weighted] + [
         lax.ppermute(weighted, "head", [(at, at ^ far) for at in range(head_devices)])
         for far in range(1, head_devices)
@@ -216,9 +276,7 @@
     grams, attended = lax.optimization_barrier((grams, attended))
     grams = lax.psum(grams, "head")
     attended, *pieces = lax.optimization_barrier((attended, *pieces))
-    for far, piece in enumerate(pieces):
-        piece_part = lax.dynamic_update_slice(piece_part, piece, (0, (own_head ^ far) * width))
-    grad_attended = dot(piece_part, out_weight, 1, 1).astype(jnp.bfloat16)
+    grad_attended = project(own_head, pieces, out_weight)
     query_grads, key_grads, value_grads = [], [], []
     for group in range(groups):
         grad_part, grad_kv = pl.pallas_call(
@@ -241,7 +299,7 @@
             ),
             name="backward",
         )(query_rows, kv_all, grad_attended, attended, log_total)
-        key_sums = lax.psum_scatter(grad_kv, "ctx", scatter_dimension=0, tiled=True)
+        key_sums = owner_sums(grad_kv, rows)
         query_grads.append(grad_part)
         key_grads.append(key_sums[:, :HD])
         value_grads.append(key_sums[:, HD:])

time: 204 us -> 186 us (0.912)
  waiting for transfers between devices: 120 us -> 42.8 us
  starting transfers between devices: 4.89 us -> 62.6 us
  Pallas kernels: 26.2 us -> 49.1 us
  matrix products: 18.3 us -> 1.66 us
  local copies, waits for them, and re-layouts: 12.7 us -> 4.72 us
  other arithmetic: 7.31 us -> 9.64 us
    reduce_scatter x2 -> x0, waiting for transfers between devices: 58.2 us -> none  [body(): key_sums = lax.psum_scatter(grad_kv, 'ctx', scatter_dimension=0, tiled=True)]
    ppermute x0 -> x8, starting transfers between devices: none -> 58 us  [swapped(): return lax.ppermute(value, 'ctx', [(at, at ^ far) for at in range(count)])]
    psum x1, waiting for transfers between devices: 27.6 us -> 0.01 us  [body(): grams = lax.psum(grams, 'head')]
    pallas_call x0 -> x1, Pallas kernels: none -> 22.9 us  [project(): pl.pallas_call(project_kernel, out_shape=jax.ShapeDtypeStruct((rows, outs...]
    dot_general x3 -> x2, matrix products: 18.3 us -> 1.66 us  [dot(): lax.dot_general(left, right, (((left_dim,), (right_dim,)), ((), ())), pre...]
    ppermute x0 -> x8, waiting for transfers between devices: none -> 8.19 us  [swapped(): return lax.ppermute(value, 'ctx', [(at, at ^ far) for at in range(count)])]
    dynamic_update_slice x4 -> x0, local copies, waits for them, and re-layouts: 6.79 us -> none  [body(): lax.dynamic_update_slice(piece_part, piece, (0, (own_head ^ far) * width))]
    squeeze x0 -> x4, local copies, waits for them, and re-layouts: none -> 4.01 us  [the longest x2 3.09 us: of_core(): return lax.dynamic_index_in_dim(blocks, index, 1, keepdims=False)]
  transfers between devices with their start and end apart: 7 -> 13, of which waited for: 5 -> 5; matrix products, arithmetic and copies ran while one was open for 17% -> 7% of each run, Pallas kernels for 13% -> 27%
where the time goes in v3:
time: 186 us; the launch traced here: 185 us
  starting transfers between devices  62.6 us (34%)
  Pallas kernels  49.1 us (26%)
  waiting for transfers between devices  42.8 us (23%)
  between operations  14.2 us (8%)
  other arithmetic  9.64 us (5%)
  local copies, waits for them, and re-layouts  4.72 us (3%)
    ppermute x8, starting transfers between devices, swapped(): return lax.ppermute(value, 'ctx', [(at, at ^ far) for at in range(count)])  58 us
    pallas_call x1, Pallas kernels, project(): pl.pallas_call(project_kernel, out_shape=jax.ShapeDtypeStruct((rows, outs...  22.9 us
    all_gather x1, waiting for transfers between devices, body(): lax.all_gather(jnp.concatenate([key_rows, value_rows], axis=1), 'ctx', ax...  22.2 us
    ppermute x3, waiting for transfers between devices, body(): lax.ppermute(weighted, 'head', [(at, at ^ far) for at in range(head_devic...  12.4 us
    pallas_call x2, Pallas kernels, body(): pl.pallas_call(functools.partial(backward_kernel, groups, group), out_sha...  11.8 us
    ppermute x8, waiting for transfers between devices, swapped(): return lax.ppermute(value, 'ctx', [(at, at ^ far) for at in range(count)])  8.19 us
    pallas_call x1, Pallas kernels, body(): pl.pallas_call(functools.partial(forward_kernel, groups), out_shape=(jax....  7.58 us
    pallas_call x1, Pallas kernels, body(): pl.pallas_call(functools.partial(squares_kernel, heads), out_shape=jax.Sh...  6.84 us
  transfers between devices with their start and end apart: 13, of which 5 were waited for; matrix products, arithmetic and copies ran while one was open for 7% of the time, Pallas kernels for 27%

profile of v3, /device:TPU:0, one launch (start us, length us, event | category | flops | bytes accessed | tf_op | source)
XLA Modules:
  0.0 184.8 jit_solution(2261221397366548015)
XLA Ops:
  7.2 1.8 pad_maximum_fusion.1
  9.1 0.7 convert_add_fusion.4
  9.7 1.5 multiply_convert_fusion.refs_0_
  11.2 3.0 %collective-permute-start = (bf16[256,2048]{1,0:T(8,128)(2,1)S(1)}, bf16[256,2048]{1,0:T(8,128)(2,1)S(1)}, u32[]{:S(2)}, u32[]{:S(2)}) collective-permute-start(bf16[256,2048]{1,0:T(8,128)(2,1)S(1)} %multiply_convert_fusion.refs_0_), channel_id=1, source_target_pairs={{0,1},{1,0},{2,3},{3,2},{4,5},{5,4},{6,7},{7,6},{8,9},{9,8},{10,11... | collective-permute-start | bytes 3145736 | tf_op jit(solution)/shard_map/ppermute | solution.py:249
  14.2 1.5 collective-permute-start.1
  15.8 0.5 fusion.11
  16.3 1.2 fusion.10
  17.4 1.8 pad_maximum_fusion
  19.2 22.2 %all-gather.2.cloned.1.call-done.kv_ref = bf16[2048,512]{1,0:T(8,128)(2,1)} async-done(((bf16[256,512]{1,0:T(8,128)(2,1)}), bf16[2048,512]{1,0:T(8,128)(2,1)}) %all-gather.2.cloned.1.call-update) | async-done | bytes 2097168 | tf_op jit(solution)/shard_map/all_gather | solution.py:243
  41.5 7.6 %forward.1 = (bf16[2048,256]{1,0:T(8,128)(2,1)}, f32[16,256]{1,0:T(8,128)}) custom-call(bf16[256,2048]{1,0:T(8,128)(2,1)} %query_ref.5, bf16[2048,512]{1,0:T(8,128)(2,1)} %all-gather.2.cloned.1.call-done.kv_ref), custom_call_target="tpu_custom_call" | custom-call | flops 8589934592 | bytes 8388608 | tf_op jit(solution)/shard_map/forward/pallas_call | solution.py:257
  49.0 12.4 %collective-permute-done.1.refs_2_ = bf16[256,2048]{1,0:T(8,128)(2,1)} collective-permute-done((bf16[256,2048]{1,0:T(8,128)(2,1)S(1)}, bf16[256,2048]{1,0:T(8,128)(2,1)}, u32[]{:S(2)}, u32[]{:S(2)}) %collective-permute-start.1) | collective-permute-done | bytes 1048608 | tf_op jit(solution)/shard_map/ppermute | solution.py:249
  61.5 22.9 %project.1.grad_ref = bf16[256,2048]{1,0:T(8,128)(2,1)} custom-call(s32[1]{0:T(128)} %bitcast.own_ref, bf16[256,2048]{1,0:T(8,128)(2,1)} %copy-done.1, bf16[256,2048]{1,0:T(8,128)(2,1)} %copy-done.3, bf16[256,2048]{1,0:T(8,128)(2,1)} %collective-permute-done.1.refs_2_, bf16[256,2048]{1,0:T(8,128)(2,1)} %collective-permute-done.2.refs_3_, ...), custom_call_target="tpu_custom_call" | custom-call | tf_op jit(solution)/shard_map/project/pallas_call | solution.py:199
  84.4 6.0 %backward.2 = (bf16[256,1024]{1,0:T(8,128)(2,1)}, bf16[2048,256]{1,0:T(8,128)(2,1)}) custom-call(bf16[256,2048]{1,0:T(8,128)(2,1)} %query_ref.5, bf16[2048,512]{1,0:T(8,128)(2,1)} %all-gather.2.cloned.1.call-done.kv_ref, bf16[256,2048]{1,0:T(8,128)(2,1)} %project.1.grad_ref, bf16[2048,256]{1,0:T(8,128)(2,1)} %get-tuple-element.24.attended_ref, ...), custom_call_target="tpu_custom_call" | custom-call | flops 10737418240 | bytes 8388608 | tf_op jit(solution)/shard_map/backward/pallas_call | solution.py:282
  90.3 1.1 dynamic-slice_bitcast_fusion.1
  91.4 0.9 collective-permute-start.3
  92.3 5.8 %backward.3 = (bf16[256,1024]{1,0:T(8,128)(2,1)}, bf16[2048,256]{1,0:T(8,128)(2,1)}) custom-call(bf16[256,2048]{1,0:T(8,128)(2,1)} %query_ref.5, bf16[2048,512]{1,0:T(8,128)(2,1)} %all-gather.2.cloned.1.call-done.kv_ref, bf16[256,2048]{1,0:T(8,128)(2,1)} %project.1.grad_ref, bf16[2048,256]{1,0:T(8,128)(2,1)} %get-tuple-element.24.attended_ref, ...), custom_call_target="tpu_custom_call" | custom-call | flops 10737418240 | bytes 8388608 | tf_op jit(solution)/shard_map/backward/pallas_call | solution.py:282
  98.2 2.0 %dynamic-slice_bitcast_fusion = bf16[4,256,256]{2,1,0:T(8,128)(2,1)} fusion(bf16[4,2,256,256]{3,2,1,0:T(8,128)(2,1)} %bitcast.43, s32[]{:T(128)S(6)} %select_n.42), kind=kLoop, calls=%fused_computation.6 | loop fusion | bytes 1048580 | tf_op jit(solution)/shard_map/jit(dynamic_index_in_dim)/squeeze | solution.py:222
  100.2 2.1 %collective-permute-start.7 = (bf16[4,256,256]{2,1,0:T(8,128)(2,1)}, bf16[4,256,256]{2,1,0:T(8,128)(2,1)S(1)}, u32[]{:S(2)}, u32[]{:S(2)}) collective-permute-start(bf16[4,256,256]{2,1,0:T(8,128)(2,1)} %dynamic-slice_bitcast_fusion), channel_id=1, source_target_pairs={{0,4},{4,0},{8,12},{12,8},{16,20},{20,16},{24,28},{28,24},{1,5},{5... | collective-permute-start | bytes 1572872 | tf_op jit(solution)/shard_map/ppermute | solution.py:225
  102.5 0.9 dynamic-slice_bitcast_fusion.7
  103.3 14.0 %collective-permute-start.4 = (bf16[256,256]{1,0:T(8,128)(2,1)}, bf16[256,256]{1,0:T(8,128)(2,1)S(1)}, u32[]{:S(2)}, u32[]{:S(2)}) collective-permute-start(bf16[256,256]{1,0:T(8,128)(2,1)} %get-tuple-element.31), channel_id=1, source_target_pairs={{0,8},{4,12},{8,0},{12,4},{16,24},{20,28},{24,16},{28,20},{1,9},{5... | collective-permute-start | bytes 393224 | tf_op jit(solution)/shard_map/ppermute | solution.py:225
  117.4 36.6 %collective-permute-start.5 = (bf16[256,256]{1,0:T(8,128)(2,1)}, bf16[256,256]{1,0:T(8,128)(2,1)S(1)}, u32[]{:S(2)}, u32[]{:S(2)}) collective-permute-start(bf16[256,256]{1,0:T(8,128)(2,1)} %get-tuple-element.33), channel_id=1, source_target_pairs={{0,16},{4,20},{8,24},{12,28},{16,0},{20,4},{24,8},{28,12},{1,17},{... | collective-permute-start | bytes 393224 | tf_op jit(solution)/shard_map/ppermute | solution.py:225
  153.9 6.8 %squares.1 = f32[32,256]{1,0:T(8,128)} custom-call(bf16[256,2048]{1,0:T(8,128)(2,1)} %copy-done.2, bf16[2048,256]{1,0:T(8,128)(2,1)} %get-tuple-element.24.attended_ref, f32[512,256]{1,0:T(8,128)} %all-reduce.2.cloned.1.call-done.gram_ref), custom_call_target="tpu_custom_call" | custom-call | tf_op jit(solution)/shard_map/squares/pallas_call | solution.py:309
  160.8 0.9 reduce_sum.9
  161.7 1.2 fusion
  162.9 3.9 %collective-permute-start.10 = (bf16[256,256]{1,0:T(8,128)(2,1)S(1)}, bf16[256,256]{1,0:T(8,128)(2,1)S(1)}, u32[]{:S(2)}, u32[]{:S(2)}) collective-permute-start(bf16[256,256]{1,0:T(8,128)(2,1)S(1)} %get-tuple-element.35), channel_id=1, source_target_pairs={{0,24},{4,28},{8,16},{12,20},{16,8},{20,12},{24,0},{28,4},{1,25},{... | collective-permute-start | bytes 393224 | tf_op jit(solution)/shard_map/ppermute | solution.py:225
  166.8 0.6 slice_bitcast_fusion
  167.4 0.6 collective-permute-start.9
  168.0 1.0 fusion.7
  169.0 2.1 %collective-permute-done.10 = bf16[256,256]{1,0:T(8,128)(2,1)S(1)} collective-permute-done((bf16[256,256]{1,0:T(8,128)(2,1)S(1)}, bf16[256,256]{1,0:T(8,128)(2,1)S(1)}, u32[]{:S(2)}, u32[]{:S(2)}) %collective-permute-start.10) | collective-permute-done | bytes 131104 | tf_op jit(solution)/shard_map/ppermute | solution.py:225
  171.1 2.1 %collective-permute-done.8 = bf16[256,256]{1,0:T(8,128)(2,1)S(1)} collective-permute-done((bf16[256,256]{1,0:T(8,128)(2,1)S(1)}, bf16[256,256]{1,0:T(8,128)(2,1)S(1)}, u32[]{:S(2)}, u32[]{:S(2)}) %collective-permute-start.8) | collective-permute-done | bytes 131104 | tf_op jit(solution)/shard_map/ppermute | solution.py:225
  173.2 4.0 %collective-permute-done.9 = bf16[256,256]{1,0:T(8,128)(2,1)S(1)} collective-permute-done((bf16[256,256]{1,0:T(8,128)(2,1)S(1)}, bf16[256,256]{1,0:T(8,128)(2,1)S(1)}, u32[]{:S(2)}, u32[]{:S(2)}) %collective-permute-start.9) | collective-permute-done | bytes 131104 | tf_op jit(solution)/shard_map/ppermute | solution.py:225
  177.3 0.7 pad_maximum_fusion.2
  (37 shorter events, 0.5 us)
Async XLA Ops:
  7.2 9.1 %copy-start = (bf16[256,2048]{1,0:T(8,128)(2,1)S(1)}, bf16[256,2048]{1,0:T(8,128)(2,1)}, u32[]{:S(2)}) copy-start(bf16[256,2048]{1,0:T(8,128)(2,1)} %param.7) | copy-start | bytes 3145732
  7.2 34.3 %all-gather.2.cloned.1.call-start = ((), (), s32[]{:S(2)}) async-start(), calls=%async_computation | async-start | bytes 2359296 | tf_op jit(solution)/shard_map/all_gather | solution.py:243
  9.0 144.9 %all-reduce.2.cloned.1.call-start = ((), (), s32[]{:S(2)}) async-start(), calls=%async_computation.1 | async-start | bytes 1048576 | tf_op jit(solution)/shard_map/psum | solution.py:277
  11.2 6.2 %copy-start.1 = (bf16[256,2048]{1,0:T(8,128)(2,1)}, bf16[256,2048]{1,0:T(8,128)(2,1)S(1)}, u32[]{:S(2)}) copy-start(bf16[256,2048]{1,0:T(8,128)(2,1)S(1)} %multiply_convert_fusion.refs_0_) | copy-start | bytes 3145732
  11.2 37.8 %collective-permute-start = (bf16[256,2048]{1,0:T(8,128)(2,1)S(1)}, bf16[256,2048]{1,0:T(8,128)(2,1)S(1)}, u32[]{:S(2)}, u32[]{:S(2)}) collective-permute-start(bf16[256,2048]{1,0:T(8,128)(2,1)S(1)} %multiply_convert_fusion.refs_0_), channel_id=1, source_target_pairs={{0,1},{1,0},{2,3},{3,2},{4,5},{5,4},{6,7},{7,6},{8,9},{9,8},{10,11... | collective-permute-start | bytes 3145736 | tf_op jit(solution)/shard_map/ppermute | solution.py:249
  14.2 47.2 %collective-permute-start.1 = (bf16[256,2048]{1,0:T(8,128)(2,1)S(1)}, bf16[256,2048]{1,0:T(8,128)(2,1)}, u32[]{:S(2)}, u32[]{:S(2)}) collective-permute-start(bf16[256,2048]{1,0:T(8,128)(2,1)S(1)} %multiply_convert_fusion.refs_0_), channel_id=1, source_target_pairs={{0,2},{1,3},{2,0},{3,1},{4,6},{5,7},{6,4},{7,5},{8,10},{9,11},{10,... | collective-permute-start | bytes 3145736 | tf_op jit(solution)/shard_map/ppermute | solution.py:249
  15.7 45.7 %collective-permute-start.2 = (bf16[256,2048]{1,0:T(8,128)(2,1)S(1)}, bf16[256,2048]{1,0:T(8,128)(2,1)}, u32[]{:S(2)}, u32[]{:S(2)}) collective-permute-start(bf16[256,2048]{1,0:T(8,128)(2,1)S(1)} %multiply_convert_fusion.refs_0_), channel_id=1, source_target_pairs={{0,3},{1,2},{2,1},{3,0},{4,7},{5,6},{6,5},{7,4},{8,11},{9,10},{10,... | collective-permute-start | bytes 3145736 | tf_op jit(solution)/shard_map/ppermute | solution.py:249
  49.0 12.4 %copy-start.3 = (bf16[256,2048]{1,0:T(8,128)(2,1)}, bf16[256,2048]{1,0:T(8,128)(2,1)S(1)}, u32[]{:S(2)}) copy-start(bf16[256,2048]{1,0:T(8,128)(2,1)S(1)} %collective-permute-done.refs_1_) | copy-start | bytes 3145732
  91.4 6.7 %copy-start.6 = (bf16[256,1024]{1,0:T(8,128)(2,1)S(1)}, bf16[256,1024]{1,0:T(8,128)(2,1)}, u32[]{:S(2)}) copy-start(bf16[256,1024]{1,0:T(8,128)(2,1)} %get-tuple-element.26) | copy-start | bytes 1572868
  91.4 10.9 %collective-permute-start.3 = (bf16[4,256,256]{2,1,0:T(8,128)(2,1)S(1)}, bf16[4,256,256]{2,1,0:T(8,128)(2,1)S(1)}, u32[]{:S(2)}, u32[]{:S(2)}) collective-permute-start(bf16[4,256,256]{2,1,0:T(8,128)(2,1)S(1)} %dynamic-slice_bitcast_fusion.1), channel_id=1, source_target_pairs={{0,4},{4,0},{8,12},{12,8},{16,20},{20,16},{24,28},{28,24},{1,5},{5... | collective-permute-start | bytes 1572872 | tf_op jit(solution)/shard_map/ppermute | solution.py:225
  98.1 4.1 %copy-start.5 = (bf16[256,1024]{1,0:T(8,128)(2,1)S(1)}, bf16[256,1024]{1,0:T(8,128)(2,1)}, u32[]{:S(2)}) copy-start(bf16[256,1024]{1,0:T(8,128)(2,1)} %get-tuple-element.27) | copy-start | bytes 1572868
  98.1 4.2 %copy-start.4 = (bf16[2048,256]{1,0:T(8,128)(2,1)S(1)}, bf16[2048,256]{1,0:T(8,128)(2,1)}, u32[]{:S(2)}) copy-start(bf16[2048,256]{1,0:T(8,128)(2,1)} %get-tuple-element.28) | copy-start | bytes 3145732
  100.2 61.5 %collective-permute-start.7 = (bf16[4,256,256]{2,1,0:T(8,128)(2,1)}, bf16[4,256,256]{2,1,0:T(8,128)(2,1)S(1)}, u32[]{:S(2)}, u32[]{:S(2)}) collective-permute-start(bf16[4,256,256]{2,1,0:T(8,128)(2,1)} %dynamic-slice_bitcast_fusion), channel_id=1, source_target_pairs={{0,4},{4,0},{8,12},{12,8},{16,20},{20,16},{24,28},{28,24},{1,5},{5... | collective-permute-start | bytes 1572872 | tf_op jit(solution)/shard_map/ppermute | solution.py:225
  102.3 51.6 %copy-start.2 = (bf16[256,2048]{1,0:T(8,128)(2,1)}, bf16[256,2048]{1,0:T(8,128)(2,1)S(1)}, u32[]{:S(2)}) copy-start(bf16[256,2048]{1,0:T(8,128)(2,1)S(1)} %constant_dynamic-update-slice_fusion.grad_query_ref) | copy-start | bytes 3145732
  103.3 64.0 %collective-permute-start.4 = (bf16[256,256]{1,0:T(8,128)(2,1)}, bf16[256,256]{1,0:T(8,128)(2,1)S(1)}, u32[]{:S(2)}, u32[]{:S(2)}) collective-permute-start(bf16[256,256]{1,0:T(8,128)(2,1)} %get-tuple-element.31), channel_id=1, source_target_pairs={{0,8},{4,12},{8,0},{12,4},{16,24},{20,28},{24,16},{28,20},{1,9},{5... | collective-permute-start | bytes 393224 | tf_op jit(solution)/shard_map/ppermute | solution.py:225
  117.4 50.6 %collective-permute-start.5 = (bf16[256,256]{1,0:T(8,128)(2,1)}, bf16[256,256]{1,0:T(8,128)(2,1)S(1)}, u32[]{:S(2)}, u32[]{:S(2)}) collective-permute-start(bf16[256,256]{1,0:T(8,128)(2,1)} %get-tuple-element.33), channel_id=1, source_target_pairs={{0,16},{4,20},{8,24},{12,28},{16,0},{20,4},{24,8},{28,12},{1,17},{... | collective-permute-start | bytes 393224 | tf_op jit(solution)/shard_map/ppermute | solution.py:225
  153.9 14.1 %collective-permute-start.6 = (bf16[256,256]{1,0:T(8,128)(2,1)S(1)}, bf16[256,256]{1,0:T(8,128)(2,1)}, u32[]{:S(2)}, u32[]{:S(2)}) collective-permute-start(bf16[256,256]{1,0:T(8,128)(2,1)S(1)} %get-tuple-element.32), channel_id=1, source_target_pairs={{0,24},{4,28},{8,16},{12,20},{16,8},{20,12},{24,0},{28,4},{1,25},{... | collective-permute-start | bytes 393224 | tf_op jit(solution)/shard_map/ppermute | solution.py:225
  162.9 8.2 %collective-permute-start.10 = (bf16[256,256]{1,0:T(8,128)(2,1)S(1)}, bf16[256,256]{1,0:T(8,128)(2,1)S(1)}, u32[]{:S(2)}, u32[]{:S(2)}) collective-permute-start(bf16[256,256]{1,0:T(8,128)(2,1)S(1)} %get-tuple-element.35), channel_id=1, source_target_pairs={{0,24},{4,28},{8,16},{12,20},{16,8},{20,12},{24,0},{28,4},{1,25},{... | collective-permute-start | bytes 393224 | tf_op jit(solution)/shard_map/ppermute | solution.py:225
  166.8 6.4 %collective-permute-start.8 = (bf16[256,256]{1,0:T(8,128)(2,1)S(1)}, bf16[256,256]{1,0:T(8,128)(2,1)S(1)}, u32[]{:S(2)}, u32[]{:S(2)}) collective-permute-start(bf16[256,256]{1,0:T(8,128)(2,1)S(1)} %get-tuple-element.34), channel_id=1, source_target_pairs={{0,8},{4,12},{8,0},{12,4},{16,24},{20,28},{24,16},{28,20},{1,9},{5... | collective-permute-start | bytes 393224 | tf_op jit(solution)/shard_map/ppermute | solution.py:225
  167.4 9.8 %collective-permute-start.9 = (bf16[256,256]{1,0:T(8,128)(2,1)S(1)}, bf16[256,256]{1,0:T(8,128)(2,1)S(1)}, u32[]{:S(2)}, u32[]{:S(2)}) collective-permute-start(bf16[256,256]{1,0:T(8,128)(2,1)S(1)} %get-tuple-element.36), channel_id=1, source_target_pairs={{0,16},{4,20},{8,24},{12,28},{16,0},{20,4},{24,8},{28,12},{1,17},{... | collective-permute-start | bytes 393224 | tf_op jit(solution)/shard_map/ppermute | solution.py:225
Sparse Core Ops, SparseCore 0:
  9.6 31.7 all-gather.1
  61.6 65.8 all-reduce.1
